TPU v7x, 32 devices: a whole 2x2x4 slice. The times are simulated.
32 devices in a mesh: dp: 16 (over z, y, core), tensor: 2 (over x).
Axes of the slice: x: 2, y: 2, z: 4, core: 2. Of those that a mesh axis runs over, the one named last changes fastest.
Arguments:
- tokens: bfloat16 [32768, 768], P('dp'), may hold values from -6 to 6
- lengths: int32 [16, 8], P('dp'), may hold values from 1 to 1344, 1792 in all within a row
- qkv_weight: bfloat16 [3, 768, 768], P(None, None, 'tensor'), may hold values from -0.21875 to 0.21875
- qkv_bias: bfloat16 [2, 768], P(None, 'tensor'), may hold values from -3 to 3
- out_weight: bfloat16 [768, 768], P('tensor'), may hold values from -1.75 to 1.75
- out_bias: bfloat16 [768], replicated, may hold values from -3 to 3
- up_weight: bfloat16 [768, 3072], P(None, 'tensor'), may hold values from -0.21875 to 0.21875
- up_bias: bfloat16 [3072], P('tensor'), may hold values from -3 to 3
- down_weight: bfloat16 [3072, 768], P('tensor'), may hold values from -0.109375 to 0.109375
- down_bias: bfloat16 [768], replicated, may hold values from -3 to 3
- norm_gains: float32 [2, 768], replicated, may hold values from 0.5 to 1.5
- norm_biases: float32 [2, 768], replicated, may hold values from -2 to 2
- cotangent: bfloat16 [32768, 768], P('dp'), may hold values from -6 to 6
Outputs:
- output: bfloat16 [32768, 768], P('dp')
- input_grad: bfloat16 [32768, 768], P('dp')
- grad_qkv_weight: float32 [3, 768, 768], P(None, None, 'tensor')
- grad_qkv_bias: float32 [2, 768], P(None, 'tensor')
- grad_out_weight: float32 [768, 768], P('tensor')
- grad_out_bias: float32 [768], replicated
- grad_up_weight: float32 [768, 3072], P(None, 'tensor')
- grad_up_bias: float32 [3072], P('tensor')
- grad_down_weight: float32 [3072, 768], P('tensor')
- grad_down_bias: float32 [768], replicated
- grad_norm_gains: float32 [2, 768], replicated
- grad_norm_biases: float32 [2, 768], replicated
Inputs may be any that keep to these rules, and one draw needn't show every extreme that they name: Each row's lengths sum to 1792, one of them is exactly 1344; the last 256 tokens of each row are padding.
All inputs are finite; a program needn't handle non-finite values.
Results may differ from a plain program's by a relative error of at most 0.0072.
Values sent between devices are 32-bit elements; how exact they have to be, the bound alone decides.
A program may use at most 256 MiB of HBM per device.

v0:
```python
import jax
import jax.numpy as jnp
from jax import lax
from jax.sharding import PartitionSpec as P

HEAD = 64
ROT = 16


epsilon = 1e-05
rot_base = 10000.0


def layout(lengths_row, length):
    slots = lengths_row.shape[0]
    seg_ends = jnp.cumsum(lengths_row, dtype=jnp.int32)
    seg_starts = seg_ends - lengths_row
    places = jnp.arange(length, dtype=jnp.int32)
    segment = jnp.sum(
        (places[:, None] >= seg_ends[None, :]).astype(jnp.int32), axis=1, dtype=jnp.int32
    )
    member = segment[:, None] == jnp.arange(slots, dtype=jnp.int32)[None, :]
    first = jnp.sum(jnp.where(member, seg_starts[None, :], 0), axis=1, dtype=jnp.int32)
    padded = segment >= slots
    position = jnp.where(padded, 0, places - first)
    segment = jnp.where(padded, slots + places, segment)
    return (segment, position)


def angles(position):
    half = ROT // 2
    frequency = rot_base ** (-(2.0 * jnp.arange(half, dtype=jnp.float32)) / ROT)
    theta = position.astype(jnp.float32)[:, None] * frequency[None, :]
    return (jnp.cos(theta), jnp.sin(theta))


def rotate(values, cosine, sine):
    half = ROT // 2
    first_half = values[..., :half]
    second_half = values[..., half:ROT]
    cosine = cosine[:, None, :]
    sine = sine[:, None, :]
    return jnp.concatenate(
        [
            first_half * cosine - second_half * sine,
            second_half * cosine + first_half * sine,
            values[..., ROT:],
        ],
        axis=-1,
    )


def unrotate(grads, cosine, sine):
    half = ROT // 2
    first_half = grads[..., :half]
    second_half = grads[..., half:ROT]
    cosine = cosine[:, None, :]
    sine = sine[:, None, :]
    return jnp.concatenate(
        [
            first_half * cosine + second_half * sine,
            second_half * cosine - first_half * sine,
            grads[..., ROT:],
        ],
        axis=-1,
    )


def normalize(values, gain, shift):
    average = jnp.mean(values, axis=-1, keepdims=True)
    centered = values - average
    inverse = lax.rsqrt(jnp.mean(centered * centered, axis=-1, keepdims=True) + epsilon)
    normal_hat = centered * inverse
    return (normal_hat * gain + shift, normal_hat, inverse)


def norm_back(incoming, normal_hat, inverse, gain):
    scaled = incoming * gain
    return inverse * (
        scaled
        - jnp.mean(scaled, axis=-1, keepdims=True)
        - normal_hat * jnp.mean(scaled * normal_hat, axis=-1, keepdims=True)
    )


def masked_scores(query_block, keys, seg_block, place_block, segment, places, scale):
    scores = (
        jnp.einsum("qhd,khd->hqk", query_block, keys, preferred_element_type=jnp.float32) * scale
    )
    allowed = (seg_block[:, None] == segment[None, :]) & (places[None, :] <= place_block[:, None])
    return jnp.where(allowed[None], scores, -1e30)


def attend_forward(query, keys, values, segment, scale):
    length, head_count, head_size = query.shape
    block = min(512, length)
    steps = length // block
    places = jnp.arange(length, dtype=jnp.int32)

    def one_block(items):
        query_block, seg_block, place_block = items
        scores = masked_scores(query_block, keys, seg_block, place_block, segment, places, scale)
        peak = jnp.max(scores, axis=-1, keepdims=True)
        raised = jnp.exp(scores - peak)
        row_total = jnp.sum(raised, axis=-1, keepdims=True)
        probabilities = (raised / row_total).astype(jnp.bfloat16)
        result = jnp.einsum(
            "hqk,khd->qhd", probabilities, values, preferred_element_type=jnp.float32
        )
        return (result, (peak + jnp.log(row_total))[..., 0])

    attended, log_total = lax.map(
        one_block,
        (
            query.reshape(steps, block, head_count, head_size),
            segment.reshape(steps, block),
            places.reshape(steps, block),
        ),
    )
    return (attended.reshape(length, head_count, head_size), log_total)


def attend_back(query, keys, values, segment, log_total, attended_grad, scale):
    length, head_count, head_size = query.shape
    block = min(512, length)
    steps = length // block
    places = jnp.arange(length, dtype=jnp.int32)

    def one_block(carry, items):
        key_acc, value_acc = carry
        query_block, seg_block, place_block, log_block, grad_block = items
        scores = masked_scores(query_block, keys, seg_block, place_block, segment, places, scale)
        probabilities = jnp.exp(scores - log_block[..., None])
        prob_low = probabilities.astype(jnp.bfloat16)
        value_acc = value_acc + jnp.einsum(
            "hqk,qhd->khd", prob_low, grad_block, preferred_element_type=jnp.float32
        )
        prob_grad = jnp.einsum(
            "qhd,khd->hqk", grad_block, values, preferred_element_type=jnp.float32
        )
        row_dot = jnp.sum(probabilities * prob_grad, axis=-1, keepdims=True)
        score_grad = (probabilities * (prob_grad - row_dot)).astype(jnp.bfloat16)
        query_part = (
            jnp.einsum("hqk,khd->qhd", score_grad, keys, preferred_element_type=jnp.float32) * scale
        )
        key_acc = (
            key_acc
            + jnp.einsum(
                "hqk,qhd->khd", score_grad, query_block, preferred_element_type=jnp.float32
            )
            * scale
        )
        return ((key_acc, value_acc), query_part)

    empty = jnp.zeros((length, head_count, head_size), jnp.float32)
    items = (
        query.reshape(steps, block, head_count, head_size),
        segment.reshape(steps, block),
        places.reshape(steps, block),
        log_total,
        attended_grad.reshape(steps, block, head_count, head_size),
    )
    (key_grad, value_grad), query_grad = lax.scan(one_block, (empty, empty), items)
    return (query_grad.reshape(length, head_count, head_size), key_grad, value_grad)


def per_device(
    tokens,
    lengths,
    qkv_weight,
    qkv_bias,
    out_weight,
    out_bias,
    up_weight,
    up_bias,
    down_weight,
    down_bias,
    norm_gains,
    norm_biases,
    cotangent,
):
    length = tokens.shape[0]
    local_width = qkv_weight.shape[2]
    head_count = local_width // HEAD
    scale = HEAD ** (-0.5)
    segment, position = layout(lengths[0], length)
    cosine, sine = angles(position)
    inputs = tokens.astype(jnp.float32)
    first_norm, first_hat, first_inv = normalize(inputs, norm_gains[0], norm_biases[0])
    first_low = first_norm.astype(jnp.bfloat16)
    projected = jnp.einsum("td,cde->cte", first_low, qkv_weight, preferred_element_type=jnp.float32)
    query_pre = projected[0] + qkv_bias[0].astype(jnp.float32)
    key_pre = projected[1]
    value_low = (
        (projected[2] + qkv_bias[1].astype(jnp.float32))
        .astype(jnp.bfloat16)
        .reshape(length, head_count, HEAD)
    )
    query_low = rotate(query_pre.reshape(length, head_count, HEAD), cosine, sine).astype(
        jnp.bfloat16
    )
    key_low = rotate(key_pre.reshape(length, head_count, HEAD), cosine, sine).astype(jnp.bfloat16)
    attended, log_total = attend_forward(query_low, key_low, value_low, segment, scale)
    attended_low = attended.reshape(length, local_width).astype(jnp.bfloat16)
    second_norm, second_hat, second_inv = normalize(inputs, norm_gains[1], norm_biases[1])
    second_low = second_norm.astype(jnp.bfloat16)
    hidden_pre = jnp.dot(
        second_low, up_weight, preferred_element_type=jnp.float32
    ) + up_bias.astype(jnp.float32)
    active_low = jax.nn.gelu(hidden_pre, approximate=False).astype(jnp.bfloat16)
    partial_value = jnp.dot(attended_low, out_weight, preferred_element_type=jnp.float32) + jnp.dot(
        active_low, down_weight, preferred_element_type=jnp.float32
    )
    summed = lax.psum(partial_value, "tensor")
    output = (
        inputs + summed + out_bias.astype(jnp.float32) + down_bias.astype(jnp.float32)
    ).astype(jnp.bfloat16)
    upstream = cotangent.astype(jnp.float32)
    bias_grad = jnp.sum(upstream, axis=0)
    active_grad = jnp.einsum(
        "td,fd->tf", cotangent, down_weight, preferred_element_type=jnp.float32
    )
    down_grad = jnp.einsum("tf,td->fd", active_low, cotangent, preferred_element_type=jnp.float32)
    gelu_value, gelu_pull = jax.vjp(lambda hid: jax.nn.gelu(hid, approximate=False), hidden_pre)
    hidden_grad = gelu_pull(active_grad)[0].astype(jnp.bfloat16)
    up_grad = jnp.einsum("td,tf->df", second_low, hidden_grad, preferred_element_type=jnp.float32)
    up_bias_grad = jnp.sum(hidden_grad.astype(jnp.float32), axis=0)
    second_grad = jnp.einsum(
        "tf,df->td", hidden_grad, up_weight, preferred_element_type=jnp.float32
    )
    proj_out_grad = jnp.einsum(
        "te,td->ed", attended_low, cotangent, preferred_element_type=jnp.float32
    )
    attended_grad = jnp.einsum(
        "td,ed->te", cotangent, out_weight, preferred_element_type=jnp.float32
    ).astype(jnp.bfloat16)
    query_grad, key_grad, value_grad = attend_back(
        query_low,
        key_low,
        value_low,
        segment,
        log_total,
        attended_grad.reshape(length, head_count, HEAD),
        scale,
    )
    query_low_grad = (
        unrotate(query_grad, cosine, sine).reshape(length, local_width).astype(jnp.bfloat16)
    )
    key_low_grad = (
        unrotate(key_grad, cosine, sine).reshape(length, local_width).astype(jnp.bfloat16)
    )
    value_low_grad = value_grad.reshape(length, local_width).astype(jnp.bfloat16)
    proj_grads = jnp.stack([query_low_grad, key_low_grad, value_low_grad])
    qkv_grad = jnp.einsum("td,cte->cde", first_low, proj_grads, preferred_element_type=jnp.float32)
    qkv_bias_grad = jnp.stack(
        [
            jnp.sum(query_low_grad.astype(jnp.float32), axis=0),
            jnp.sum(value_low_grad.astype(jnp.float32), axis=0),
        ]
    )
    first_grad = jnp.einsum(
        "cte,cde->td", proj_grads, qkv_weight, preferred_element_type=jnp.float32
    )
    first_full, second_full = lax.psum((first_grad, second_grad), "tensor")
    gain_grad = jnp.stack(
        [jnp.sum(first_full * first_hat, axis=0), jnp.sum(second_full * second_hat, axis=0)]
    )
    shift_grad = jnp.stack([jnp.sum(first_full, axis=0), jnp.sum(second_full, axis=0)])
    shares = norm_back(first_full, first_hat, first_inv, norm_gains[0]) + norm_back(
        second_full, second_hat, second_inv, norm_gains[1]
    )
    input_grad = (upstream + shares).astype(jnp.bfloat16)
    (
        qkv_grad,
        qkv_bias_grad,
        proj_out_grad,
        up_grad,
        up_bias_grad,
        down_grad,
        bias_grad,
        gain_grad,
        shift_grad,
    ) = lax.psum(
        (
            qkv_grad,
            qkv_bias_grad,
            proj_out_grad,
            up_grad,
            up_bias_grad,
            down_grad,
            bias_grad,
            gain_grad,
            shift_grad,
        ),
        "dp",
    )
    return (
        output,
        input_grad,
        qkv_grad,
        qkv_bias_grad,
        proj_out_grad,
        bias_grad,
        up_grad,
        up_bias_grad,
        down_grad,
        bias_grad,
        gain_grad,
        shift_grad,
    )


def solution(mesh):
    in_specs = (
        P("dp", None),
        P("dp", None),
        P(None, None, "tensor"),
        P(None, "tensor"),
        P("tensor", None),
        P(),
        P(None, "tensor"),
        P("tensor"),
        P("tensor", None),
        P(),
        P(),
        P(),
        P("dp", None),
    )
    out_specs = (
        P("dp", None),
        P("dp", None),
        P(None, None, "tensor"),
        P(None, "tensor"),
        P("tensor", None),
        P(),
        P(None, "tensor"),
        P("tensor"),
        P("tensor", None),
        P(),
        P(),
        P(),
    )
    return jax.shard_map(
        per_device, mesh=mesh, in_specs=in_specs, out_specs=out_specs, check_vma=False
    )
```

profile of v0, /device:TPU:0, one launch (start us, length us, event | category | flops | bytes accessed | tf_op | source)
XLA Modules:
  0.0 1560.0 jit_solution(579964785994693710)
XLA Ops:
  14.6 4.7 convolution_bitcast_fusion
  19.3 3.9 fusion.85
  43.9 164.9 %while.28 = (s32[]{:T(128)}, bf16[4,512,6,64]{1,3,2,0:T(8,128)(2,1)}, f32[4,6,512]{2,1,0:T(8,128)}, s32[4,512]{1,0:T(4,128)S(1)}, s32[2048]{0:T(1024)S(1)}, /*in...) while((s32[]{:T(128)}, ...), condition=%wide.region_8.9_spmd.clone, body=%wide.region_5.8_spmd.clone.sunk | while | flops 1689252864 | bytes 90433160 | solution.py:112
  46.0 14.3 fusion.136
  60.3 12.1 fusion.137
  73.0 12.3 fusion.138
  87.2 14.3 fusion.136
  101.5 12.1 fusion.137
  114.1 12.3 fusion.138
  128.3 14.3 fusion.136
  142.6 12.1 fusion.137
  155.3 12.3 fusion.138
  169.5 14.3 fusion.136
  183.8 12.1 fusion.137
  196.5 12.3 fusion.138
  208.8 4.9 convolution_convert_fusion
  216.3 3.9 reshape_reshape.4
  223.1 440.5 %while.29 = (s32[]{:T(128)}, f32[2048,6,64]{0,2,1:T(8,128)}, f32[2048,6,64]{0,2,1:T(8,128)}, f32[4,512,6,64]{1,0,3,2:T(4,128)}, bf16[4,512,6,64]{1,3,2,0:T(8,128...) while((s32[]{:T(128)}, f32[2048,6,64]{0,2,1:T(8,128)}, ...), condition=%wide.region_12.13_spmd.clone, body=%wide.region_10.12_spmd.clone.sunk | while | flops 4128175104 | bytes 215853216 | solution.py:163
  237.5 13.3 fusion.148
  251.6 18.1 %multiply_reduce_fusion.4 = (f32[6,512]{1,0:T(8,128)S(1)}, f32[6,512,2048]{2,1,0:T(8,128)}) fusion(f32[6,512,2048]{2,1,0:T(8,128)} %fusion.148, f32[6,512]{1,0:T(8,128)S(1)} %dynamic-slice_bitcast_fusion.2, pred[512,2048]{1,0:T(8,128)(4,1)S(1)} %fusion.149, bf16[2048,6,64]{0,2,1:T(8,128)(2,1)} %get-tuple-element.598, ...), kind=kOutput, calls=%fused_computation.22.clone.1 | convolution fusion | flops 836760576 | bytes 53371392 | tf_op jit(solution)/shard_map/while/body/eval_jaxpr/qhd,khd->hqk/dot_general | solution.py:138
  269.7 21.3 %multiply_convert_fusion.3 = bf16[6,512,2048]{2,1,0:T(8,128)(2,1)} fusion(f32[6,512,2048]{2,1,0:T(8,128)} %get-tuple-element.527, f32[6,512,2048]{2,1,0:T(8,128)} %fusion.148, f32[6,512]{1,0:T(8,128)S(1)} %get-tuple-element.528, f32[6,512]{1,0:T(8,128)S(1)} %dynamic-slice_bitcast_fusion.2, pred[512,2048]{1,0:T(8,128)(4,1)S(1)} %fusion.149), kind=kLoop, calls=%fused_computation.21.clone.1 | loop fusion | flops 37748736 | bytes 63987712 | tf_op jit(solution)/shard_map/while/body/eval_jaxpr/convert_element_type | solution.py:142
  290.9 9.8 fusion.150
  303.6 16.1 %dynamic_update_slice.21 = f32[4,512,6,64]{1,0,3,2:T(4,128)} dynamic-update-slice(f32[4,512,6,64]{1,0,3,2:T(4,128)} %get-tuple-element.576, f32[1,512,6,64]{1,0,3,2:T(1,128)} %copy.85, s32[]{:T(128)} %get-tuple-element.573, s32[]{:T(128)} %constant.64.clone.1..sunk, s32[]{:T(128)} %constant.64.clone.1..sunk, s32[]{:T(128)} %constant.64.clone.1..sunk) | dynamic-update-slice | bytes 1572868 | tf_op jit(solution)/shard_map/while/body/jit(dynamic_update_index_in_dim)/dynamic_update_slice | solution.py:112
  319.7 8.7 bitcast_add_fusion.4
  328.4 12.8 bitcast_add_fusion.5
  343.1 13.3 fusion.148
  357.1 18.1 %multiply_reduce_fusion.4 = (f32[6,512]{1,0:T(8,128)S(1)}, f32[6,512,2048]{2,1,0:T(8,128)}) fusion(f32[6,512,2048]{2,1,0:T(8,128)} %fusion.148, f32[6,512]{1,0:T(8,128)S(1)} %dynamic-slice_bitcast_fusion.2, pred[512,2048]{1,0:T(8,128)(4,1)S(1)} %fusion.149, bf16[2048,6,64]{0,2,1:T(8,128)(2,1)} %get-tuple-element.598, ...), kind=kOutput, calls=%fused_computation.22.clone.1 | convolution fusion | flops 836760576 | bytes 53371392 | tf_op jit(solution)/shard_map/while/body/eval_jaxpr/qhd,khd->hqk/dot_general | solution.py:138
  375.2 21.3 %multiply_convert_fusion.3 = bf16[6,512,2048]{2,1,0:T(8,128)(2,1)} fusion(f32[6,512,2048]{2,1,0:T(8,128)} %get-tuple-element.527, f32[6,512,2048]{2,1,0:T(8,128)} %fusion.148, f32[6,512]{1,0:T(8,128)S(1)} %get-tuple-element.528, f32[6,512]{1,0:T(8,128)S(1)} %dynamic-slice_bitcast_fusion.2, pred[512,2048]{1,0:T(8,128)(4,1)S(1)} %fusion.149), kind=kLoop, calls=%fused_computation.21.clone.1 | loop fusion | flops 37748736 | bytes 63987712 | tf_op jit(solution)/shard_map/while/body/eval_jaxpr/convert_element_type | solution.py:142
  396.5 9.8 fusion.150
  409.2 16.1 %dynamic_update_slice.21 = f32[4,512,6,64]{1,0,3,2:T(4,128)} dynamic-update-slice(f32[4,512,6,64]{1,0,3,2:T(4,128)} %get-tuple-element.576, f32[1,512,6,64]{1,0,3,2:T(1,128)} %copy.85, s32[]{:T(128)} %get-tuple-element.573, s32[]{:T(128)} %constant.64.clone.1..sunk, s32[]{:T(128)} %constant.64.clone.1..sunk, s32[]{:T(128)} %constant.64.clone.1..sunk) | dynamic-update-slice | bytes 1572868 | tf_op jit(solution)/shard_map/while/body/jit(dynamic_update_index_in_dim)/dynamic_update_slice | solution.py:112
  425.3 9.6 bitcast_add_fusion.4
  434.9 13.7 bitcast_add_fusion.5
  450.5 13.3 fusion.148
  464.5 18.1 %multiply_reduce_fusion.4 = (f32[6,512]{1,0:T(8,128)S(1)}, f32[6,512,2048]{2,1,0:T(8,128)}) fusion(f32[6,512,2048]{2,1,0:T(8,128)} %fusion.148, f32[6,512]{1,0:T(8,128)S(1)} %dynamic-slice_bitcast_fusion.2, pred[512,2048]{1,0:T(8,128)(4,1)S(1)} %fusion.149, bf16[2048,6,64]{0,2,1:T(8,128)(2,1)} %get-tuple-element.598, ...), kind=kOutput, calls=%fused_computation.22.clone.1 | convolution fusion | flops 836760576 | bytes 53371392 | tf_op jit(solution)/shard_map/while/body/eval_jaxpr/qhd,khd->hqk/dot_general | solution.py:138
  482.6 21.3 %multiply_convert_fusion.3 = bf16[6,512,2048]{2,1,0:T(8,128)(2,1)} fusion(f32[6,512,2048]{2,1,0:T(8,128)} %get-tuple-element.527, f32[6,512,2048]{2,1,0:T(8,128)} %fusion.148, f32[6,512]{1,0:T(8,128)S(1)} %get-tuple-element.528, f32[6,512]{1,0:T(8,128)S(1)} %dynamic-slice_bitcast_fusion.2, pred[512,2048]{1,0:T(8,128)(4,1)S(1)} %fusion.149), kind=kLoop, calls=%fused_computation.21.clone.1 | loop fusion | flops 37748736 | bytes 63987712 | tf_op jit(solution)/shard_map/while/body/eval_jaxpr/convert_element_type | solution.py:142
  503.8 9.8 fusion.150
  516.5 16.1 %dynamic_update_slice.21 = f32[4,512,6,64]{1,0,3,2:T(4,128)} dynamic-update-slice(f32[4,512,6,64]{1,0,3,2:T(4,128)} %get-tuple-element.576, f32[1,512,6,64]{1,0,3,2:T(1,128)} %copy.85, s32[]{:T(128)} %get-tuple-element.573, s32[]{:T(128)} %constant.64.clone.1..sunk, s32[]{:T(128)} %constant.64.clone.1..sunk, s32[]{:T(128)} %constant.64.clone.1..sunk) | dynamic-update-slice | bytes 1572868 | tf_op jit(solution)/shard_map/while/body/jit(dynamic_update_index_in_dim)/dynamic_update_slice | solution.py:112
  532.6 9.6 bitcast_add_fusion.4
  542.2 13.7 bitcast_add_fusion.5
  557.8 13.3 fusion.148
  571.8 18.1 %multiply_reduce_fusion.4 = (f32[6,512]{1,0:T(8,128)S(1)}, f32[6,512,2048]{2,1,0:T(8,128)}) fusion(f32[6,512,2048]{2,1,0:T(8,128)} %fusion.148, f32[6,512]{1,0:T(8,128)S(1)} %dynamic-slice_bitcast_fusion.2, pred[512,2048]{1,0:T(8,128)(4,1)S(1)} %fusion.149, bf16[2048,6,64]{0,2,1:T(8,128)(2,1)} %get-tuple-element.598, ...), kind=kOutput, calls=%fused_computation.22.clone.1 | convolution fusion | flops 836760576 | bytes 53371392 | tf_op jit(solution)/shard_map/while/body/eval_jaxpr/qhd,khd->hqk/dot_general | solution.py:138
  589.9 21.3 %multiply_convert_fusion.3 = bf16[6,512,2048]{2,1,0:T(8,128)(2,1)} fusion(f32[6,512,2048]{2,1,0:T(8,128)} %get-tuple-element.527, f32[6,512,2048]{2,1,0:T(8,128)} %fusion.148, f32[6,512]{1,0:T(8,128)S(1)} %get-tuple-element.528, f32[6,512]{1,0:T(8,128)S(1)} %dynamic-slice_bitcast_fusion.2, pred[512,2048]{1,0:T(8,128)(4,1)S(1)} %fusion.149), kind=kLoop, calls=%fused_computation.21.clone.1 | loop fusion | flops 37748736 | bytes 63987712 | tf_op jit(solution)/shard_map/while/body/eval_jaxpr/convert_element_type | solution.py:142
  611.2 9.8 fusion.150
  623.8 16.1 %dynamic_update_slice.21 = f32[4,512,6,64]{1,0,3,2:T(4,128)} dynamic-update-slice(f32[4,512,6,64]{1,0,3,2:T(4,128)} %get-tuple-element.576, f32[1,512,6,64]{1,0,3,2:T(1,128)} %copy.85, s32[]{:T(128)} %get-tuple-element.573, s32[]{:T(128)} %constant.64.clone.1..sunk, s32[]{:T(128)} %constant.64.clone.1..sunk, s32[]{:T(128)} %constant.64.clone.1..sunk) | dynamic-update-slice | bytes 1572868 | tf_op jit(solution)/shard_map/while/body/jit(dynamic_update_index_in_dim)/dynamic_update_slice | solution.py:112
  639.9 9.6 bitcast_add_fusion.4
  649.5 13.7 bitcast_add_fusion.5
  663.6 5.3 reshape.355
  685.1 3.8 convert_reduce_fusion.3
  698.4 34.7 %multiply_convert_fusion.1 = (bf16[2048,1536]{1,0:T(8,128)(2,1)}, f32[2048,1536]{1,0:T(8,128)}, f32[2048,1536]{1,0:T(8,128)}) fusion(f32[1536]{0:T(1024)S(1)} %convert_element_type.130, bf16[768,1536]{1,0:T(8,128)(2,1)S(1)} %copy-done, bf16[2048,768]{1,0:T(8,128)(2,1)S(1)} %copy-done.3, f32[768]{0:T(1024)S(1)} %copy-done.39, f32[768]{0:T(1024)S(1)} %copy-done.28, ...), kind=kOutput, calls=%fused_computation.56 | convolution fusion | flops 5048893440 | bytes 36990976 | tf_op jit(solution)/shard_map/dot_general | solution.py:207
  733.1 16.2 %convert_reduce_fusion = (f32[1536]{0:T(1024)S(1)}, bf16[2048,1536]{1,0:T(8,128)(2,1)}) fusion(f32[2048,1536]{1,0:T(8,128)} %get-tuple-element.349, bf16[2048,768]{1,0:T(8,128)(2,1)S(1)} %copy-done.9, bf16[1536,768]{1,0:T(8,128)(2,1)} %param.25, f32[2048,1536]{1,0:T(8,128)} %get-tuple-element.378, f32[1536]{0:T(1024)S(1)} %convert_element_type.130), kind=kOutput, calls=%fused_computation.54 | convolution fusion | flops 4885314048 | bytes 36974592 | tf_op jit(solution)/shard_map/td,fd->tf/dot_general | solution.py:220
  749.3 10.7 fusion.80
  760.0 6.9 fusion.89
  766.9 6.6 convolution_bitcast_fusion.2
  773.6 8.2 fusion.86
  781.8 5.0 convolution_add_fusion
  786.9 6.2 convolution_bitcast_fusion.1
  793.1 7.0 fusion.87
  801.0 234.0 %all-reduce.6.cloned.1.call-done = (f32[3,768,384]{1,2,0:T(8,128)}, f32[384,768]{1,0:T(8,128)}, f32[768,1536]{1,0:T(8,128)}, f32[1536,768]{1,0:T(8,128)}) async-done(((f32[3,768,384]{1,2,0:T(8,128)}, f32[384,768]{1,0:T(8,128)}, f32[768,1536]{1,0:T(8,128)}, f32[1536,768]{1,0:T(8,128)}), (f32[3,768,384]{1,2,0:T(8,128)}, f32[384,768]{1,0:T(8,128)}, f32[768,1536]{1,0:T(8,128)}, ...) | async-done | bytes 14155792 | tf_op jit(solution)/shard_map/psum | solution.py:283
  1034.9 5.2 copy.60
  1040.1 422.5 %all-reduce.8.cloned.1.call-done = (f32[2048,768]{1,0:T(8,128)}, f32[2048,768]{1,0:T(8,128)}, f32[2048,768]{1,0:T(8,128)}) async-done(((f32[2048,768]{1,0:T(8,128)}, f32[2048,768]{1,0:T(8,128)}, f32[2048,768]{1,0:T(8,128)}), (f32[2048,768]{1,0:T(8,128)}, f32[2048,768]{1,0:T(8,128)}, f32[2048,768]{1,0:T(8,128)})) %all-reduce.8.cloned.1.call-update) | async-done | bytes 18874384 | tf_op jit(solution)/shard_map/psum | solution.py:214
  1462.6 8.2 fusion.67
  1472.7 8.8 convert_reduce_fusion.2
  1481.4 61.3 %all-reduce = (f32[2,384]{1,0:T(2,128)}, f32[768]{0:T(1024)S(1)}, f32[1536]{0:T(1024)}, f32[2,768]{1,0:T(2,128)}, f32[2,768]{1,0:T(2,128)}) all-reduce(f32[2,384]{1,0:T(2,128)S(1)} %pad_maximum_fusion.7, f32[768]{0:T(1024)S(1)} %get-tuple-element.369, f32[1536]{0:T(1024)S(1)} %get-tuple-element.379, ...), channel_id=1, replica_groups=mesh['dp'=16,'tensor'=2] {'dp'}, use_global_device_ids=true, to_apply=%region_22.23 | all-reduce | flops 6144 | bytes 49152 | tf_op jit(solution)/shard_map/psum | solution.py:283
  1545.7 5.0 copy.122
  (206 shorter events, 98.9 us)
Async XLA Ops:
  7.2 691.2 %copy-start = (bf16[768,1536]{1,0:T(8,128)(2,1)S(1)}, bf16[768,1536]{1,0:T(8,128)(2,1)}, u32[]{:S(2)}) copy-start(bf16[768,1536]{1,0:T(8,128)(2,1)} %param.23) | copy-start | bytes 7077892
  7.2 6.1 copy-start.34
  7.2 6.1 copy-start.33
  7.2 1027.7 %all-reduce.6.cloned.1.call-start = ((), (), s32[]{:S(2)}) async-start(), calls=%async_computation | async-start | bytes 28311552 | tf_op jit(solution)/shard_map/psum | solution.py:283
  7.8 6.8 copy-start.2
  7.8 6.8 copy-start.43
  10.3 3.7 copy-start.24
  13.4 0.6 copy-start.26
  14.0 0.6 copy-start.29
  14.0 5.3 copy-start.37
  19.3 4.0 copy-start.35
  19.3 4.1 copy-start.45
  30.5 2.1 copy-start.16
  30.5 2.1 copy-start.18
  34.0 8.7 copy-start.20
  34.0 8.7 copy-start.21
  43.9 164.9 %copy-start.22 = (bf16[384,768]{1,0:T(8,128)(2,1)S(1)}, bf16[384,768]{1,0:T(8,128)(2,1)}, u32[]{:S(2)}) copy-start(bf16[384,768]{1,0:T(8,128)(2,1)} %param.21) | copy-start | bytes 1769476
  60.3 12.7 copy-start.1
  101.5 12.7 copy-start.1
  142.6 12.7 copy-start.1
  183.8 12.7 copy-start.1
  663.6 7.1 copy-start.17
  663.6 7.1 copy-start.19
  685.1 9.7 copy-start.36
  691.5 4.4 copy-start.9
  694.3 4.1 copy-start.3
  694.3 4.1 copy-start.25
  694.3 4.1 copy-start.27
  694.3 4.0 copy-start.28
  694.3 4.0 copy-start.39
  694.8 1.1 copy-start.7
  749.3 10.7 copy-start.46
  760.0 6.9 copy-start.10
  760.0 6.9 copy-start.12
  760.0 6.9 copy-start.14
  760.0 6.9 copy-start.30
  760.0 6.9 copy-start.38
  773.5 8.3 copy-start.23
  773.5 689.1 %all-reduce.8.cloned.1.call-start = ((), (), s32[]{:S(2)}) async-start(), calls=%async_computation.1 | async-start | bytes 37748736 | tf_op jit(solution)/shard_map/psum | solution.py:214
  773.5 8.2 copy-start.8
  781.8 5.1 copy-start.11
  781.8 5.1 copy-start.13
  781.8 5.1 copy-start.15
  781.8 5.1 copy-start.44
  781.8 11.2 slice-start.2
  786.9 6.2 slice-start.3
  800.1 0.7 copy-start.31
  800.1 0.8 copy-start.32
  800.1 0.8 copy-start.41
  800.1 0.8 copy-start.42
  1462.6 8.4 copy-start.4
  1462.6 8.4 copy-start.5
  1462.6 10.1 copy-start.6
  1481.4 69.3 %slice-start = ((s8[4718592]{0:T(1024)(128)(4,1)}), s8[524288]{0:T(1024)(128)(4,1)S(1)}, s32[]{:S(2)}) async-start(s8[4718592]{0:T(1024)(128)(4,1)} %bitcast.156), calls=%async_computation.2 | async-start | bytes 1048576
  1542.8 10.2 copy-start.40
  1545.7 5.0 slice-start.1
Sparse Core Ops, SparseCore 0:
  773.6 261.3 all-reduce.5
  1037.7 424.8 all-reduce.7
where the time goes:
time: 1560 us
  waiting for transfers between devices  657 us (42%)
  matrix products  476 us (31%)
  other arithmetic  191 us (12%)
  local copies, waits for them, and re-layouts  147 us (9%)
  blocking collectives  61.3 us (4%)
    psum x1, waiting for transfers between devices, per_device(): summed = lax.psum(partial_value, 'tensor')  422 us
    psum x1, waiting for transfers between devices, per_device(): lax.psum((qkv_grad, qkv_bias_grad, proj_out_grad, up_grad, up_bias_grad,...  234 us
    dot_general x8, matrix products, masked_scores(): jnp.einsum('qhd,khd->hqk', query_block, keys, preferred_element_type=jnp....  110 us
    convert_element_type x4, other arithmetic, one_block(): score_grad = (probabilities * (prob_grad - row_dot)).astype(jnp.bfloat16)  85.1 us
    dynamic_update_slice x8, local copies, waits for them, and re-layouts, attend_forward(): lax.map(one_block, (query.reshape(steps, block, head_count, head_size), s...  75.9 us
    dot_general x4, matrix products, one_block(): jnp.einsum('qhd,khd->hqk', grad_block, values, preferred_element_type=jnp...  72.4 us
    psum x1, blocking collectives, per_device(): lax.psum((qkv_grad, qkv_bias_grad, proj_out_grad, up_grad, up_bias_grad,...  61.3 us
    dot_general x4, matrix products, one_block(): jnp.einsum('hqk,qhd->khd', prob_low, grad_block, preferred_element_type=j...  53.8 us
  transfers between devices with their start and end apart: 2, of which 2 were waited for; matrix products, arithmetic and copies ran while one was open for 2% of the time, Pallas kernels for 0%

commit v1 on v0

v1 whole, which is shorter than its diff:
```python
import functools
import math

import jax
import jax.numpy as jnp
import numpy as np
from jax import lax
from jax.experimental import pallas as pl
from jax.experimental.pallas import tpu as pltpu
from jax.sharding import PartitionSpec as P

HEAD = 64
ROT = 16
HALF = ROT // 2
epsilon = 1e-05
rot_base = 10000.0
f32 = jnp.float32
bf16 = jnp.bfloat16
NN = (((1,), (0,)), ((), ()))
NT = (((1,), (1,)), ((), ()))
TN = (((0,), (0,)), ((), ()))
TT = (((0,), (1,)), ((), ()))
VMEM_LIMIT = 60 * 2**20


def dot(a, b, dims=NN):
    return lax.dot_general(a, b, dims, preferred_element_type=f32)


def whole(shape):
    zeros = (0,) * len(shape)
    return pl.BlockSpec(shape, lambda *_: zeros, pipeline_mode=pl.Buffered(1))


def once(shape):
    zeros = (0,) * len(shape)
    return pl.BlockSpec(shape, lambda *_: zeros)


def hat_of(values):
    average = jnp.mean(values, axis=-1, keepdims=True)
    centered = values - average
    inverse = lax.rsqrt(jnp.mean(centered * centered, axis=-1, keepdims=True) + epsilon)
    return centered * inverse, inverse


def gelu_pair(h):
    a = jnp.abs(h) * np.float32(math.sqrt(0.5))
    t = 1.0 / (1.0 + np.float32(0.3275911) * a)
    bell = jnp.exp(-0.5 * (h * h))
    poly = np.float32(0.5 * 1.061405429) * t + np.float32(0.5 * -1.453152027)
    poly = poly * t + np.float32(0.5 * 1.421413741)
    poly = poly * t + np.float32(0.5 * -0.284496736)
    poly = poly * t + np.float32(0.5 * 0.254829592)
    tail = poly * t * bell
    phi = jnp.where(h >= 0, 1.0 - tail, tail)
    return h * phi, phi + h * bell * np.float32(1.0 / math.sqrt(2.0 * math.pi))


def add_to(ref, first, value):
    @pl.when(first)
    def _():
        ref[...] = value

    @pl.when(jnp.logical_not(first))
    def _():
        ref[...] += value


def mlp_kernel(chunk, tok, g, up, upb, down, gains, biases, part, share, dup, ddown, small, upb_sum):
    i = pl.program_id(0)
    hat, _ = hat_of(tok[...].astype(f32))
    gain = gains[1:2, :]
    normed = (hat * gain + biases[1:2, :]).astype(bf16)
    gt = g[...]
    total = None
    back = None
    wide = up.shape[1]

    @pl.when(i == 0)
    def _():
        dup[...] = jnp.zeros_like(dup)
        ddown[...] = jnp.zeros_like(ddown)
        small[...] = jnp.zeros_like(small)
        upb_sum[...] = jnp.zeros_like(upb_sum)

    for c in range(wide // chunk):
        sl = slice(c * chunk, (c + 1) * chunk)
        hidden = dot(normed, up[:, sl]) + upb[:, sl]
        act_grad = dot(gt, down[sl, :], NT)
        act, slope = gelu_pair(hidden)
        act = act.astype(bf16)
        hid_grad = (act_grad * slope).astype(bf16)
        p = dot(act, down[sl, :])
        e = dot(hid_grad, up[:, sl], NT)
        total = p if total is None else total + p
        back = e if back is None else back + e
        dup[:, sl] += dot(normed, hid_grad, TN)
        ddown[sl, :] += dot(act, gt, TN)
        upb_sum[:, sl] += jnp.sum(hid_grad.astype(f32), axis=0, keepdims=True)
    part[...] = total
    share[...] = back * gain
    small[0:1, :] += jnp.sum(gt.astype(f32), axis=0, keepdims=True)
    small[1:2, :] += jnp.sum(back * hat, axis=0, keepdims=True)
    small[2:3, :] += jnp.sum(back, axis=0, keepdims=True)


def mlp(tok, g, up, upb, down, gains, biases, tile=256, chunk=512):
    length, d = tok.shape
    wide = up.shape[1]
    rows = pl.BlockSpec((tile, d), lambda i: (i, 0))
    return pl.pallas_call(
        functools.partial(mlp_kernel, chunk),
        grid=(length // tile,),
        in_specs=[rows, rows, whole((d, wide)), whole((1, wide)), whole((wide, d)), whole((2, d)), whole((2, d))],
        out_specs=[rows, rows, once((d, wide)), once((wide, d)), once((8, d)), once((1, wide))],
        out_shape=[
            jax.ShapeDtypeStruct((length, d), f32),
            jax.ShapeDtypeStruct((length, d), f32),
            jax.ShapeDtypeStruct((d, wide), f32),
            jax.ShapeDtypeStruct((wide, d), f32),
            jax.ShapeDtypeStruct((8, d), f32),
            jax.ShapeDtypeStruct((1, wide), f32),
        ],
        compiler_params=pltpu.CompilerParams(vmem_limit_bytes=VMEM_LIMIT),
        cost_estimate=pl.CostEstimate(flops=12 * length * d * wide, bytes_accessed=4 * length * d * 4, transcendentals=0),
        name="mlp",
    )(tok, g, up, upb, down, gains, biases)


def first_tokens(lens, places):
    first = jnp.zeros_like(places)
    end = lens[0, 0]
    for j in range(1, lens.shape[1]):
        first = jnp.where(places >= end, end, first)
        end = end + lens[0, j]
    return jnp.where(places >= end, places, first)


def turn(block, cosine, sine, sign):
    parts = []
    for h in range(block.shape[0] // HEAD):
        r = h * HEAD
        a = block[r : r + HALF, :]
        b = block[r + HALF : r + ROT, :]
        if sign > 0:
            parts += [a * cosine - b * sine, b * cosine + a * sine]
        else:
            parts += [a * cosine + b * sine, b * cosine - a * sine]
        parts.append(block[r + ROT : r + HEAD, :])
    return jnp.concatenate(parts, axis=0)


def proj_kernel(lens, tok, g, w, bias, ow, gains, biases, freq, qt, q, kt, k, vt, dot_t, do, cosine, sine):
    tile = tok.shape[0]
    i = pl.program_id(0)
    hat, _ = hat_of(tok[...].astype(f32))
    normed = (hat * gains[0:1, :] + biases[0:1, :]).astype(bf16)
    places = i * tile + lax.broadcasted_iota(jnp.int32, (1, tile), 1)
    position = (places - first_tokens(lens, places)).astype(f32)
    theta = freq[:, 0:1] * position
    c = jnp.cos(theta)
    s = jnp.sin(theta)
    cosine[...] = c
    sine[...] = s
    scale = HEAD ** (-0.5)
    query = turn(dot(w[0], normed, TT) + bias[:, 0:1], c, s, 1).astype(bf16) * scale
    qt[...] = query
    q[...] = query.T
    key = turn(dot(w[1], normed, TT), c, s, 1).astype(bf16)
    kt[...] = key
    k[...] = key.T
    vt[...] = (dot(w[2], normed, TT) + bias[:, 1:2]).astype(bf16)
    grad = dot(ow[...], g[...], NT).astype(bf16)
    dot_t[...] = grad
    do[...] = grad.T


def project(lens, tok, g, w, bias, ow, gains, biases, freq, tile=512):
    length, d = tok.shape
    e = w.shape[2]
    rows = pl.BlockSpec((tile, d), lambda i, *_: (i, 0))
    tr = pl.BlockSpec((e, tile), lambda i, *_: (0, i))
    nat = pl.BlockSpec((tile, e), lambda i, *_: (i, 0))
    ang = pl.BlockSpec((HALF, tile), lambda i, *_: (0, i))
    t_shape = jax.ShapeDtypeStruct((e, length), bf16)
    n_shape = jax.ShapeDtypeStruct((length, e), bf16)
    a_shape = jax.ShapeDtypeStruct((HALF, length), f32)
    return pl.pallas_call(
        proj_kernel,
        grid_spec=pltpu.PrefetchScalarGridSpec(
            num_scalar_prefetch=1,
            grid=(length // tile,),
            in_specs=[rows, rows, whole((3, d, e)), whole((e, 2)), whole((e, d)), whole((2, d)), whole((2, d)), whole((HALF, 128))],
            out_specs=[tr, nat, tr, nat, tr, tr, nat, ang, ang],
        ),
        out_shape=[t_shape, n_shape, t_shape, n_shape, t_shape, t_shape, n_shape, a_shape, a_shape],
        compiler_params=pltpu.CompilerParams(vmem_limit_bytes=VMEM_LIMIT),
        cost_estimate=pl.CostEstimate(flops=8 * length * d * e, bytes_accessed=20 * length * e, transcendentals=0),
        name="project",
    )(lens, tok, g, w, bias, ow, gains, biases, freq)


def tile_range(lens, start):
    first = jnp.int32(0)
    end = lens[0, 0]
    for j in range(1, lens.shape[1]):
        first = jnp.where(start >= end, end, first)
        end = end + lens[0, j]
    return jnp.where(start >= end, start, first)


def attend_kernel(tk, lens, qt, k, vt, dot_t, ot, lse, delta, qpad, m_s, l_s, acc):
    i = pl.program_id(0)
    tq = qt.shape[1]
    heads = qt.shape[0] // HEAD
    q0 = i * tq
    places = q0 + lax.broadcasted_iota(jnp.int32, (1, tq), 1)
    first = first_tokens(lens, places)
    zero = jnp.zeros((HEAD, tq), bf16)
    for h in range(heads):
        qh = qt[h * HEAD : (h + 1) * HEAD, :]
        qpad[h] = jnp.concatenate([qh, zero] if h % 2 == 0 else [zero, qh], axis=0)
    m_s[...] = jnp.full_like(m_s, -1e30)
    l_s[...] = jnp.zeros_like(l_s)
    acc[...] = jnp.zeros_like(acc)
    low = lax.div(tile_range(lens, q0), tk)
    high = lax.div(q0 + tq + tk - 1, tk)

    def step(j, carry):
        k0 = pl.multiple_of(j * tk, tk)
        rows = k0 + lax.broadcasted_iota(jnp.int32, (tk, tq), 0)
        allowed = (rows >= first) & (rows <= places)
        for h in range(heads):
            pair = (h // 2) * 128
            s = dot(k[pl.ds(k0, tk), pair : pair + 128], qpad[h])
            s = jnp.where(allowed, s, -1e30)
            m_old = m_s[h : h + 1, :]
            m_new = jnp.maximum(m_old, jnp.max(s, axis=0, keepdims=True))
            p = jnp.exp(s - m_new)
            alpha = jnp.exp(m_old - m_new)
            m_s[h : h + 1, :] = m_new
            l_s[h : h + 1, :] = l_s[h : h + 1, :] * alpha + jnp.sum(p, axis=0, keepdims=True)
            o = dot(vt[h * HEAD : (h + 1) * HEAD, pl.ds(k0, tk)], p.astype(bf16))
            acc[h * HEAD : (h + 1) * HEAD, :] = acc[h * HEAD : (h + 1) * HEAD, :] * alpha + o
        return carry

    lax.fori_loop(low, high, step, 0)
    lse[...] = m_s[...] + jnp.log(l_s[...])
    for h in range(heads):
        sl = slice(h * HEAD, (h + 1) * HEAD)
        o = acc[sl, :] / l_s[h : h + 1, :]
        ot[sl, :] = o.astype(bf16)
        delta[h : h + 1, :] = jnp.sum(o * dot_t[sl, :].astype(f32), axis=0, keepdims=True)


def attend(lens, qt, k, vt, dot_t, tq=256, tk=256):
    e, length = qt.shape
    heads = e // HEAD
    cols = pl.BlockSpec((e, tq), lambda i, *_: (0, i))
    stat = pl.BlockSpec((8, tq), lambda i, *_: (0, i))
    return pl.pallas_call(
        functools.partial(attend_kernel, tk),
        grid_spec=pltpu.PrefetchScalarGridSpec(
            num_scalar_prefetch=1,
            grid=(length // tq,),
            in_specs=[cols, whole((length, e)), whole((e, length)), cols],
            out_specs=[cols, stat, stat],
            scratch_shapes=[
                pltpu.VMEM((heads, 128, tq), bf16),
                pltpu.VMEM((8, tq), f32),
                pltpu.VMEM((8, tq), f32),
                pltpu.VMEM((e, tq), f32),
            ],
        ),
        out_shape=[
            jax.ShapeDtypeStruct((e, length), bf16),
            jax.ShapeDtypeStruct((8, length), f32),
            jax.ShapeDtypeStruct((8, length), f32),
        ],
        compiler_params=pltpu.CompilerParams(vmem_limit_bytes=VMEM_LIMIT),
        cost_estimate=pl.CostEstimate(flops=2 * length * length * e, bytes_accessed=8 * length * e, transcendentals=0),
        name="attend",
    )(lens, qt, k, vt, dot_t)


def attend_back_kernel(tk, lens, q, qt, k, kt, vt, do, dot_t, lse, delta, cosine, sine, grads_q, grads_k, grads_v, kpad, vpad, dk, dv, dq, lse_b, del_b):
    i = pl.program_id(0)
    tq = q.shape[0]
    length = k.shape[0]
    heads = q.shape[1] // HEAD
    q0 = i * tq

    @pl.when(i == 0)
    def _():
        dk[...] = jnp.zeros_like(dk)
        dv[...] = jnp.zeros_like(dv)
        zero = jnp.zeros((HEAD, length), bf16)
        for h in range(heads):
            sl = slice(h * HEAD, (h + 1) * HEAD)
            own, other = (0, HEAD) if h % 2 == 0 else (HEAD, 0)
            kpad[h, own : own + HEAD, :] = kt[sl, :]
            kpad[h, other : other + HEAD, :] = zero
            vpad[h, own : own + HEAD, :] = vt[sl, :]
            vpad[h, other : other + HEAD, :] = zero

    places = q0 + lax.broadcasted_iota(jnp.int32, (tq, 1), 0)
    first = first_tokens(lens, places)
    lse_cols = lse[...].T
    del_cols = delta[...].T
    for h in range(heads):
        lse_b[h] = jnp.broadcast_to(lse_cols[:, h : h + 1], (tq, 128))
        del_b[h] = jnp.broadcast_to(del_cols[:, h : h + 1], (tq, 128))
    dq[...] = jnp.zeros_like(dq)
    low = lax.div(tile_range(lens, q0), tk)
    high = lax.div(q0 + tq + tk - 1, tk)

    def step(j, carry):
        k0 = pl.multiple_of(j * tk, tk)
        ks = pl.ds(k0, tk)
        cols = k0 + lax.broadcasted_iota(jnp.int32, (tq, tk), 1)
        allowed = (cols >= first) & (cols <= places)
        for h in range(heads):
            sl = slice(h * HEAD, (h + 1) * HEAD)
            pair = slice((h // 2) * 128, (h // 2) * 128 + 128)
            s = dot(q[:, pair], kpad[h, :, ks])
            s = s - jnp.concatenate([lse_b[h]] * (tk // 128), axis=1)
            p = jnp.where(allowed, jnp.exp(s), 0.0)
            dp = dot(do[:, pair], vpad[h, :, ks])
            ds = p * (dp - jnp.concatenate([del_b[h]] * (tk // 128), axis=1))
            ds = ds.astype(bf16)
            dv[sl, ks] += dot(dot_t[sl, :], p.astype(bf16))
            dk[sl, ks] += dot(qt[sl, :], ds)
            dq[h] += dot(ds, k[ks, pair])
        return carry

    lax.fori_loop(low, high, step, 0)
    scale = HEAD ** (-0.5)
    lane = lax.broadcasted_iota(jnp.int32, (tq, 128), 1)
    q_parts = [
        jnp.where(lane < HEAD, dq[2 * h], dq[2 * h + 1]).T * scale for h in range(heads // 2)
    ]
    angle = pl.ds(pl.multiple_of(q0, tq), tq)
    grads_q[...] = turn(jnp.concatenate(q_parts, axis=0), cosine[:, angle], sine[:, angle], -1).astype(bf16)

    @pl.when(i == pl.num_programs(0) - 1)
    def _():
        grads_k[...] = turn(dk[...], cosine[...], sine[...], -1).astype(bf16)
        grads_v[...] = dv[...].astype(bf16)


def attend_back(lens, q, qt, k, kt, vt, do, dot_t, lse, delta, cosine, sine, tq=256, tk=256):
    e, length = qt.shape
    heads = e // HEAD
    cols = pl.BlockSpec((e, tq), lambda i, *_: (0, i))
    rows = pl.BlockSpec((tq, e), lambda i, *_: (i, 0))
    stat = pl.BlockSpec((8, tq), lambda i, *_: (0, i))
    nat, tr, ang = whole((length, e)), whole((e, length)), whole((HALF, length))
    out = jax.ShapeDtypeStruct((e, length), bf16)
    return pl.pallas_call(
        functools.partial(attend_back_kernel, tk),
        grid_spec=pltpu.PrefetchScalarGridSpec(
            num_scalar_prefetch=1,
            grid=(length // tq,),
            in_specs=[rows, cols, nat, tr, tr, rows, cols, stat, stat, ang, ang],
            out_specs=[cols, once((e, length)), once((e, length))],
            scratch_shapes=[
                pltpu.VMEM((heads, 128, length), bf16),
                pltpu.VMEM((heads, 128, length), bf16),
                pltpu.VMEM((e, length), f32),
                pltpu.VMEM((e, length), f32),
                pltpu.VMEM((heads, tq, 128), f32),
                pltpu.VMEM((heads, tq, 128), f32),
                pltpu.VMEM((heads, tq, 128), f32),
            ],
        ),
        out_shape=[out, out, out],
        compiler_params=pltpu.CompilerParams(vmem_limit_bytes=VMEM_LIMIT),
        cost_estimate=pl.CostEstimate(flops=5 * length * length * e, bytes_accessed=20 * length * e, transcendentals=0),
        name="attend_back",
    )(lens, q, qt, k, kt, vt, do, dot_t, lse, delta, cosine, sine)


def merge_kernel(tok, g, gq, gk, gv, ot, w, ow, gains, biases, part_in, share_in, part, share, dw, dow, small, bias_sum):
    i = pl.program_id(0)
    tile = tok.shape[0]

    @pl.when(i == 0)
    def _():
        dw[...] = jnp.zeros_like(dw)
        dow[...] = jnp.zeros_like(dow)
        small[...] = jnp.zeros_like(small)
        bias_sum[...] = jnp.zeros_like(bias_sum)

    hat, _ = hat_of(tok[...].astype(f32))
    gain = gains[0:1, :]
    normed = (hat * gain + biases[0:1, :]).astype(bf16)
    back = dot(gq[...], w[0], TT) + dot(gk[...], w[1], TT) + dot(gv[...], w[2], TT)
    share[...] = share_in[...] + back * gain
    part[...] = part_in[...] + dot(ot[...], ow[...], TN)
    dw[0] += dot(normed, gq[...], TT)
    dw[1] += dot(normed, gk[...], TT)
    dw[2] += dot(normed, gv[...], TT)
    dow[...] += dot(ot[...], g[...])
    small[0:1, :] += jnp.sum(back * hat, axis=0, keepdims=True)
    small[1:2, :] += jnp.sum(back, axis=0, keepdims=True)
    ones = jnp.ones((8, tile), bf16)
    bias_sum[0] += dot(ones, gq[...], NT)
    bias_sum[1] += dot(ones, gv[...], NT)


def merge(tok, g, gq, gk, gv, ot, w, ow, gains, biases, part, share, tile=512):
    length, d = tok.shape
    e = w.shape[2]
    rows = pl.BlockSpec((tile, d), lambda i: (i, 0))
    cols = pl.BlockSpec((e, tile), lambda i: (0, i))
    full = jax.ShapeDtypeStruct((length, d), f32)
    return pl.pallas_call(
        merge_kernel,
        grid=(length // tile,),
        in_specs=[rows, rows, cols, cols, cols, cols, whole((3, d, e)), whole((e, d)), whole((2, d)), whole((2, d)), rows, rows],
        out_specs=[rows, rows, once((3, d, e)), once((e, d)), once((8, d)), once((2, 8, e))],
        out_shape=[
            full,
            full,
            jax.ShapeDtypeStruct((3, d, e), f32),
            jax.ShapeDtypeStruct((e, d), f32),
            jax.ShapeDtypeStruct((8, d), f32),
            jax.ShapeDtypeStruct((2, 8, e), f32),
        ],
        compiler_params=pltpu.CompilerParams(vmem_limit_bytes=VMEM_LIMIT),
        cost_estimate=pl.CostEstimate(flops=16 * length * d * e, bytes_accessed=24 * length * d, transcendentals=0),
        name="merge",
    )(tok, g, gq, gk, gv, ot, w, ow, gains, biases, part, share)


def per_device(
    tokens, lengths, qkv_weight, qkv_bias, out_weight, out_bias, up_weight, up_bias, down_weight, down_bias, norm_gains, norm_biases, cotangent
):
    freq = jnp.broadcast_to(
        (rot_base ** (-(2.0 * jnp.arange(HALF, dtype=f32)) / ROT))[:, None], (HALF, 128)
    )
    bias_cols = qkv_bias.astype(f32).T
    part, share, d_up, d_down, small_a, d_upb = mlp(
        tokens, cotangent, up_weight, up_bias.astype(f32)[None], down_weight, norm_gains, norm_biases
    )
    qt, q, kt, k, vt, dot_t, do, cosine, sine = project(
        lengths, tokens, cotangent, qkv_weight, bias_cols, out_weight, norm_gains, norm_biases, freq
    )
    ot, lse, delta = attend(lengths, qt, k, vt, dot_t)
    gq, gk, gv = attend_back(lengths, q, qt, k, kt, vt, do, dot_t, lse, delta, cosine, sine)
    part, share, d_qkv, d_out, small_b, bias_sum = merge(
        tokens, cotangent, gq, gk, gv, ot, qkv_weight, out_weight, norm_gains, norm_biases, part, share
    )
    summed, shares = lax.psum((part, share), "tensor")
    inputs = tokens.astype(f32)
    output = (inputs + summed + out_bias.astype(f32) + down_bias.astype(f32)).astype(bf16)
    hat, inverse = hat_of(inputs)
    input_share = inverse * (
        shares
        - jnp.mean(shares, axis=-1, keepdims=True)
        - hat * jnp.mean(shares * hat, axis=-1, keepdims=True)
    )
    input_grad = (cotangent.astype(f32) + input_share).astype(bf16)
    d_qkvb = bias_sum[:, 0, :]
    gain_shift = jnp.stack([small_b[0], small_a[1], small_b[1], small_a[2]])
    bias_grad = small_a[0]
    gain_shift = lax.psum(gain_shift, ("dp", "tensor"))
    d_qkv, d_qkvb, d_out, d_up, d_upb, d_down, bias_grad = lax.psum(
        (d_qkv, d_qkvb, d_out, d_up, d_upb, d_down, bias_grad), "dp"
    )
    return (
        output, input_grad, d_qkv, d_qkvb, d_out, bias_grad, d_up, d_upb[0], d_down, bias_grad, gain_shift[:2], gain_shift[2:],
    )


def solution(mesh):
    in_specs = (
        P("dp", None), P("dp", None), P(None, None, "tensor"), P(None, "tensor"), P("tensor", None), P(), P(None, "tensor"),
        P("tensor"), P("tensor", None), P(), P(), P(), P("dp", None),
    )
    out_specs = (
        P("dp", None), P("dp", None), P(None, None, "tensor"), P(None, "tensor"), P("tensor", None), P(), P(None, "tensor"),
        P("tensor"), P("tensor", None), P(), P(), P(),
    )
    return jax.shard_map(per_device, mesh=mesh, in_specs=in_specs, out_specs=out_specs, check_vma=False)
```

time: 1560 us -> 789 us (0.51)
  matrix products: 476 us -> 0 us
  waiting for transfers between devices: 657 us -> 442 us
  Pallas kernels: 0 us -> 185 us
  other arithmetic: 191 us -> 13.9 us
  local copies, waits for them, and re-layouts: 147 us -> 19.7 us
  blocking collectives: 61.3 us -> 115 us
    dot_general x40 -> x0, matrix products: 476 us -> none  [the longest x8 110 us: masked_scores(): jnp.einsum('qhd,khd->hqk', query_block, keys, preferred_element_type=jnp....]
    psum x2, waiting for transfers between devices: 656 us -> 441 us  [the longest x1 251 us: per_device(): lax.psum((d_qkv, d_qkvb, d_out, d_up, d_upb, d_down, bias_grad), 'dp')]
    pallas_call x0 -> x5, Pallas kernels: none -> 185 us  [the longest x1 58 us: attend_back(): pl.pallas_call(functools.partial(attend_back_kernel, tk), grid_spec=pltpu...]
    convert_element_type x9 -> x3, other arithmetic: 88.4 us -> 7.96 us  [the longest x1 7.95 us: per_device(): input_grad = (cotangent.astype(f32) + input_share).astype(bf16)]
    dynamic_update_slice x8 -> x0, local copies, waits for them, and re-layouts: 75.9 us -> none  [attend_forward(): lax.map(one_block, (query.reshape(steps, block, head_count, head_size), s...]
    reduce_sum x12 -> x3, other arithmetic: 76.7 us -> 5.84 us  [the longest x1 4.3 us: per_device(): jnp.mean(shares, axis=-1, keepdims=True)]
    psum x1 -> x2, blocking collectives: 61.3 us -> 115 us  [the longest x1 77 us: per_device(): lax.psum((d_qkv, d_qkvb, d_out, d_up, d_upb, d_down, bias_grad), 'dp')]
where the time goes in v1:
time: 789 us
  waiting for transfers between devices  442 us (56%)
  Pallas kernels  185 us (23%)
  blocking collectives  115 us (15%)
  local copies, waits for them, and re-layouts  19.7 us (2%)
  between operations  14.2 us (2%)
  other arithmetic  13.9 us (2%)
    psum x1, waiting for transfers between devices, per_device(): lax.psum((d_qkv, d_qkvb, d_out, d_up, d_upb, d_down, bias_grad), 'dp')  251 us
    psum x1, waiting for transfers between devices, per_device(): summed, shares = lax.psum((part, share), 'tensor')  190 us
    psum x1, blocking collectives, per_device(): lax.psum((d_qkv, d_qkvb, d_out, d_up, d_upb, d_down, bias_grad), 'dp')  77 us
    pallas_call x1, Pallas kernels, attend_back(): pl.pallas_call(functools.partial(attend_back_kernel, tk), grid_spec=pltpu...  58 us
    pallas_call x1, Pallas kernels, mlp(): pl.pallas_call(functools.partial(mlp_kernel, chunk), grid=(length // tile...  47.3 us
    pallas_call x1, Pallas kernels, attend(): pl.pallas_call(functools.partial(attend_kernel, tk), grid_spec=pltpu.Pref...  46 us
    psum x1, blocking collectives, per_device(): gain_shift = lax.psum(gain_shift, ('dp', 'tensor'))  37.7 us
    pallas_call x1, Pallas kernels, merge(): pl.pallas_call(merge_kernel, grid=(length // tile,), in_specs=[rows, rows...  21.9 us
  transfers between devices with their start and end apart: 2, of which 2 were waited for; matrix products, arithmetic and copies ran while one was open for 2% of the time, Pallas kernels for 0%

profile of v1, /device:TPU:0, one launch (start us, length us, event | category | flops | bytes accessed | tf_op | source)
XLA Modules:
  0.0 789.4 jit_solution(14157277350242407536)
XLA Ops:
  7.2 0.0 all-reduce.8.cloned.1.call-start
  7.2 1.5 copy.25
  8.8 1.3 reshape.53.upb
  10.0 47.3 %mlp.1 = (f32[2048,768]{1,0:T(8,128)}, f32[2048,768]{1,0:T(8,128)}, f32[768,1536]{1,0:T(8,128)}, f32[1536,768]{1,0:T(8,128)}, f32[8,768]{1,0:T(8,128)}, /*index=5*/f32[1,1536]{1,0:T(1,128)}) custom-call(bf16[2048,768]{1,0:T(8,128)(2,1)} %tok.5, bf16[2048,768]{1,0:T(8,128)(2,1)} %g.5, bf16[768,1536]{1,0:T(8,128)(2,1)} %up.1, f32[1,1536]{1,0:T(1,128)} %reshape.53.upb, ...), custom_call_target="tpu_custom_call" | custom-call | flops 28991029248 | bytes 25165824 | tf_op jit(solution)/shard_map/mlp/pallas_call | solution.py:112
  57.3 0.7 broadcast_in_dim.6.freq
  58.0 11.9 %project.1 = (bf16[384,2048]{1,0:T(8,128)(2,1)}, bf16[2048,384]{1,0:T(8,128)(2,1)}, bf16[384,2048]{1,0:T(8,128)(2,1)}, bf16[2048,384]{1,0:T(8,128)(2,1)}, bf16[3...) custom-call(s32[1,8]{1,0:T(1,128)} %lens.5, ...), custom_call_target="tpu_custom_call" | custom-call | flops 4831838208 | bytes 15728640 | tf_op jit(solution)/shard_map/project/pallas_call | solution.py:189
  69.9 46.0 %attend.1 = (bf16[384,2048]{1,0:T(8,128)(2,1)}, f32[8,2048]{1,0:T(8,128)}, f32[8,2048]{1,0:T(8,128)}) custom-call(s32[1,8]{1,0:T(1,128)} %lens.5, bf16[384,2048]{1,0:T(8,128)(2,1)} %get-tuple-element.40.qt, bf16[2048,384]{1,0:T(8,128)(2,1)} %get-tuple-element.41.k, bf16[384,2048]{1,0:T(8,128)(2,1)} %get-tuple-element.43.vt, ...), custom_call_target="tpu_custom_call" | custom-call | flops 3221225472 | bytes 6291456 | tf_op jit(solution)/shard_map/attend/pallas_call | solution.py:262
  115.9 58.0 %attend_back.1 = (bf16[384,2048]{1,0:T(8,128)(2,1)}, bf16[384,2048]{1,0:T(8,128)(2,1)}, bf16[384,2048]{1,0:T(8,128)(2,1)}) custom-call(s32[1,8]{1,0:T(1,128)} %lens.5, bf16[2048,384]{1,0:T(8,128)(2,1)} %get-tuple-element.39.q, bf16[384,2048]{1,0:T(8,128)(2,1)} %get-tuple-element.40.qt, bf16[2048,384]{1,0:T(8,128)(2,1)} %get-tuple-element.41.k, ...), custom_call_target="tpu_custom_call" | custom-call | flops 8053063680 | bytes 15728640 | tf_op jit(solution)/shard_map/attend_back/pallas_call | solution.py:360
  173.8 21.9 %merge.1 = (f32[2048,768]{1,0:T(8,128)}, f32[2048,768]{1,0:T(8,128)}, f32[3,768,384]{2,1,0:T(8,128)}, f32[384,768]{1,0:T(8,128)}, f32[8,768]{1,0:T(8,128)}, /*index=5*/f32[2,8,384]{2,1,0:T(8,128)}) custom-call(bf16[2048,768]{1,0:T(8,128)(2,1)} %tok.5, bf16[2048,768]{1,0:T(8,128)(2,1)} %g.5, bf16[384,2048]{1,0:T(8,128)(2,1)} %get-tuple-element.50.gq, ...), custom_call_target="tpu_custom_call" | custom-call | flops 9663676416 | bytes 37748736 | tf_op jit(solution)/shard_map/merge/pallas_call | solution.py:418
  195.7 0.0 all-reduce.8.cloned.1.call-update
  195.8 0.0 all-reduce.6.cloned.1.call-start
  195.8 0.0 copy-start.4
  195.8 0.0 copy-start.6
  195.8 0.0 copy-start.7
  195.8 0.0 copy-start
  195.9 0.6 all-reduce.6.cloned.1.call-update
  196.5 1.0 slice.24
  197.5 0.0 copy-done.4
  197.6 0.9 fusion.15
  198.4 77.0 %all-reduce = (f32[2,384]{1,0:T(2,128)}, f32[768]{0:T(1024)S(1)}, f32[1536]{0:T(1024)}) all-reduce(f32[2,384]{1,0:T(2,128)S(1)} %bitcast.9, f32[768]{0:T(1024)S(1)} %get-tuple-element.83, f32[1536]{0:T(1024)S(1)} %reduce.1), channel_id=1, replica_groups=mesh['dp'=16,'tensor'=2] {'dp'}, use_global_device_ids=true, to_apply=%region_7.0 | all-reduce | flops 3072 | bytes 24576 | tf_op jit(solution)/shard_map/psum | solution.py:469
  275.5 0.0 copy-start.5
  275.5 0.0 copy-done.6
  275.5 0.0 copy-done.7
  275.5 0.8 fusion.14
  276.4 37.7 %psum.79 = f32[4,768]{1,0:T(4,128)S(1)} all-reduce(f32[4,768]{1,0:T(4,128)S(1)} %pad_maximum_fusion), channel_id=1, replica_groups=mesh['dp'=16,'tensor'=2] {'dp','tensor'}, use_global_device_ids=true, to_apply=%region_13.0 | all-reduce | flops 3072 | bytes 24576 | tf_op jit(solution)/shard_map/psum | solution.py:468
  314.1 0.0 copy-done
  314.1 0.5 convert_reduce_fusion
  314.6 1.1 fusion.9
  315.7 0.6 fusion.16
  316.3 190.2 %all-reduce.8.cloned.1.call-done = (f32[2048,768]{1,0:T(8,128)}, f32[2048,768]{1,0:T(8,128)}) async-done(((f32[2048,768]{1,0:T(8,128)}, f32[2048,768]{1,0:T(8,128)}), (f32[2048,768]{1,0:T(8,128)}, f32[2048,768]{1,0:T(8,128)})) %all-reduce.8.cloned.1.call-update) | async-done | bytes 12582928 | tf_op jit(solution)/shard_map/psum | solution.py:455
  506.5 0.0 copy-start.1
  506.5 0.0 copy-start.2
  506.5 4.3 fusion.13
  510.8 0.3 copy-done.1
  511.1 0.9 copy-done.2
  512.1 7.9 %fusion.8 = (bf16[2048,768]{1,0:T(8,128)(2,1)}, bf16[2048,768]{1,0:T(8,128)(2,1)}) fusion(bf16[2048,768]{1,0:T(8,128)(2,1)S(1)} %copy-done, f32[2048,768]{1,0:T(8,128)S(1)} %copy-done.1, bf16[2048,768]{1,0:T(8,128)(2,1)S(1)} %copy-done.2, f32[2048]{0:T(1024)S(1)} %get-tuple-element.86, f32[2048]{0:T(1024)S(1)} %get-tuple-element.87, ...), kind=kLoop, calls=%fused_computation.11 | loop fusion | flops 22020096 | bytes 25204736 | tf_op jit(solution)/shard_map/convert_element_type | solution.py:464
  520.0 250.9 %all-reduce.6.cloned.1.call-done = (f32[3,768,384]{2,1,0:T(8,128)}, f32[384,768]{1,0:T(8,128)}, f32[768,1536]{1,0:T(8,128)}, f32[1536,768]{1,0:T(8,128)}) async-done(((f32[3,768,384]{2,1,0:T(8,128)}, f32[384,768]{1,0:T(8,128)}, f32[768,1536]{1,0:T(8,128)}, f32[1536,768]{1,0:T(8,128)}), (f32[3,768,384]{2,1,0:T(8,128)}, f32[384,768]{1,0:T(8,128)}, f32[768,1536]{1,0:T(8,128)}, ...) | async-done | bytes 14155792 | tf_op jit(solution)/shard_map/psum | solution.py:469
  770.9 0.0 copy-start.3
  770.9 0.0 slice-start.2
  770.9 0.0 copy-done.5
  770.9 0.6 copy.36
  771.5 0.0 slice-start.3
  771.5 4.3 copy.37
  775.8 0.0 copy-done.3
  775.8 0.0 slice-start
  775.8 1.0 copy.38
  776.8 0.0 slice-done.2
  776.8 0.0 slice-done.3
  776.8 0.0 slice-start.1
  776.8 2.4 copy.39
  779.2 0.8 slice-done
  780.0 0.3 slice-done.1
  780.4 2.2 copy.40
  (11 shorter events, 0.1 us)
Async XLA Ops:
  7.2 499.3 %all-reduce.8.cloned.1.call-start = ((), (), s32[]{:S(2)}) async-start(), calls=%async_computation.1 | async-start | bytes 25165824 | tf_op jit(solution)/shard_map/psum | solution.py:455
  195.8 575.1 %all-reduce.6.cloned.1.call-start = ((), (), s32[]{:S(2)}) async-start(), calls=%async_computation | async-start | bytes 28311552 | tf_op jit(solution)/shard_map/psum | solution.py:469
  195.8 1.7 copy-start.4
  195.8 79.7 %copy-start.6 = (bf16[768]{0:T(1024)(128)(2,1)S(1)}, bf16[768]{0:T(1024)(128)(2,1)}, u32[]{:S(2)}) copy-start(bf16[768]{0:T(1024)(128)(2,1)} %param.18) | copy-start | bytes 4612
  195.8 79.7 %copy-start.7 = (bf16[768]{0:T(1024)(128)(2,1)S(1)}, bf16[768]{0:T(1024)(128)(2,1)}, u32[]{:S(2)}) copy-start(bf16[768]{0:T(1024)(128)(2,1)} %param.22) | copy-start | bytes 4612
  195.8 118.2 %copy-start = (bf16[2048,768]{1,0:T(8,128)(2,1)S(1)}, bf16[2048,768]{1,0:T(8,128)(2,1)}, u32[]{:S(2)}) copy-start(bf16[2048,768]{1,0:T(8,128)(2,1)} %tok.5) | copy-start | bytes 9437188
  275.5 495.4 %copy-start.5 = (f32[768]{0:T(1024)}, f32[768]{0:T(1024)S(1)}, u32[]{:S(2)}) copy-start(f32[768]{0:T(1024)S(1)} %get-tuple-element.117) | copy-start | bytes 9220
  506.5 4.6 copy-start.1
  506.5 5.6 copy-start.2
  770.9 4.9 copy-start.3
  770.9 5.9 slice-start.2
  771.5 5.3 slice-start.3
  775.8 4.2 slice-start
  776.8 3.5 slice-start.1
Sparse Core Ops, SparseCore 0:
  195.9 310.5 all-reduce.7
  512.2 258.6 all-reduce.5

commit v2 on v1

v2 whole, which is shorter than its diff:
```python
import functools
import math

import jax
import jax.numpy as jnp
import numpy as np
from jax import lax
from jax.experimental import pallas as pl
from jax.experimental.pallas import tpu as pltpu
from jax.sharding import PartitionSpec as P

HEAD = 64
ROT = 16
HALF = ROT // 2
epsilon = 1e-05
rot_base = 10000.0
f32 = jnp.float32
bf16 = jnp.bfloat16
NN = (((1,), (0,)), ((), ()))
NT = (((1,), (1,)), ((), ()))
TN = (((0,), (0,)), ((), ()))
TT = (((0,), (1,)), ((), ()))
VMEM_LIMIT = 60 * 2**20


def dot(a, b, dims=NN):
    return lax.dot_general(a, b, dims, preferred_element_type=f32)


def whole(shape):
    zeros = (0,) * len(shape)
    return pl.BlockSpec(shape, lambda *_: zeros, pipeline_mode=pl.Buffered(1))


def once(shape):
    zeros = (0,) * len(shape)
    return pl.BlockSpec(shape, lambda *_: zeros)


def hat_of(values):
    average = jnp.mean(values, axis=-1, keepdims=True)
    centered = values - average
    inverse = lax.rsqrt(jnp.mean(centered * centered, axis=-1, keepdims=True) + epsilon)
    return centered * inverse, inverse


def gelu_pair(h):
    a = jnp.abs(h) * np.float32(math.sqrt(0.5))
    t = 1.0 / (1.0 + np.float32(0.3275911) * a)
    bell = jnp.exp(-0.5 * (h * h))
    poly = np.float32(0.5 * 1.061405429) * t + np.float32(0.5 * -1.453152027)
    poly = poly * t + np.float32(0.5 * 1.421413741)
    poly = poly * t + np.float32(0.5 * -0.284496736)
    poly = poly * t + np.float32(0.5 * 0.254829592)
    tail = poly * t * bell
    phi = jnp.where(h >= 0, 1.0 - tail, tail)
    return h * phi, phi + h * bell * np.float32(1.0 / math.sqrt(2.0 * math.pi))


def add_to(ref, first, value):
    @pl.when(first)
    def _():
        ref[...] = value

    @pl.when(jnp.logical_not(first))
    def _():
        ref[...] += value


def mlp_tile(chunk, tok, g, up, upb, down, gains, biases, visit):
    hat, _ = hat_of(tok[...].astype(f32))
    gain = gains[1:2, :]
    normed = (hat * gain + biases[1:2, :]).astype(bf16)
    gt = g[...]
    total = None
    back = None
    for c in range(up.shape[1] // chunk):
        sl = slice(c * chunk, (c + 1) * chunk)
        hidden = dot(normed, up[:, sl]) + upb[:, sl]
        act_grad = dot(gt, down[sl, :], NT)
        act, slope = gelu_pair(hidden)
        act = act.astype(bf16)
        hid_grad = (act_grad * slope).astype(bf16)
        p = dot(act, down[sl, :])
        e = dot(hid_grad, up[:, sl], NT)
        total = p if total is None else total + p
        back = e if back is None else back + e
        visit(sl, normed, gt, act, hid_grad)
    return hat, gt, total, back, gain


def mlp_own_kernel(chunk, meta, tok, g, up, upb, down, gains, biases, part, share, keep_d, send_d, keep_u, send_u, small, upb_sum, dup, ddown):
    i = pl.program_id(0)

    @pl.when(i == 0)
    def _():
        dup[...] = jnp.zeros_like(dup)
        ddown[...] = jnp.zeros_like(ddown)
        small[...] = jnp.zeros_like(small)
        upb_sum[...] = jnp.zeros_like(upb_sum)

    def visit(sl, normed, gt, act, hid_grad):
        dup[:, sl] += dot(normed, hid_grad, TN)
        ddown[sl, :] += dot(act, gt, TN)
        upb_sum[:, sl] += jnp.sum(hid_grad.astype(f32), axis=0, keepdims=True)

    hat, gt, total, back, gain = mlp_tile(chunk, tok, g, up, upb, down, gains, biases, visit)
    part[...] = total
    share[...] = back * gain
    small[0:1, :] += jnp.sum(gt.astype(f32), axis=0, keepdims=True)
    small[1:2, :] += jnp.sum(back * hat, axis=0, keepdims=True)
    small[2:3, :] += jnp.sum(back, axis=0, keepdims=True)

    @pl.when(i == pl.num_programs(0) - 1)
    def _():
        d, wide = dup.shape
        core = meta[0]
        for down_out, up_out, half in ((keep_d, keep_u, core), (send_d, send_u, 1 - core)):
            rows = pl.multiple_of(half * (wide // 2), wide // 2)
            down_out[...] = ddown[pl.ds(rows, wide // 2), :]
            rows = pl.multiple_of(half * (d // 2), d // 2)
            for c in range(wide // d):
                up_out[c * (d // 2) : (c + 1) * (d // 2), :] = dup[pl.ds(rows, d // 2), c * d : (c + 1) * d]


def mlp_own(meta, tok, g, up, upb, down, gains, biases, tile=512, chunk=768):
    length, d = tok.shape
    wide = up.shape[1]
    rows = pl.BlockSpec((tile, d), lambda i, *_: (i, 0))
    half = (wide // 2, d)
    shape = jax.ShapeDtypeStruct(half, f32)
    return pl.pallas_call(
        functools.partial(mlp_own_kernel, chunk),
        grid_spec=pltpu.PrefetchScalarGridSpec(
            num_scalar_prefetch=1,
            grid=(length // tile,),
            in_specs=[rows, rows, whole((d, wide)), whole((1, wide)), whole((wide, d)), whole((2, d)), whole((2, d))],
            out_specs=[rows, rows, once(half), once(half), once(half), once(half), once((8, d)), once((1, wide))],
            scratch_shapes=[pltpu.VMEM((d, wide), f32), pltpu.VMEM((wide, d), f32)],
        ),
        out_shape=[
            jax.ShapeDtypeStruct((length, d), f32),
            jax.ShapeDtypeStruct((length, d), f32),
            shape,
            shape,
            shape,
            shape,
            jax.ShapeDtypeStruct((8, d), f32),
            jax.ShapeDtypeStruct((1, wide), f32),
        ],
        compiler_params=pltpu.CompilerParams(vmem_limit_bytes=VMEM_LIMIT),
        cost_estimate=pl.CostEstimate(flops=12 * length * d * wide, bytes_accessed=4 * length * d * 4, transcendentals=0),
        name="mlp_own",
    )(meta, tok, g, up, upb, down, gains, biases)


def mlp_other_kernel(chunk, tok, g, up, upb, down, gains, biases, part_in, share_in, part, share):
    nothing = lambda *_: None
    _, _, total, back, gain = mlp_tile(chunk, tok, g, up, upb, down, gains, biases, nothing)
    part[...] = part_in[...] + total
    share[...] = share_in[...] + back * gain


def mlp_other(tok, g, up, upb, down, gains, biases, part, share, tile=512, chunk=768):
    length, d = tok.shape
    wide = up.shape[1]
    rows = pl.BlockSpec((tile, d), lambda i: (i, 0))
    full = jax.ShapeDtypeStruct((length, d), f32)
    return pl.pallas_call(
        functools.partial(mlp_other_kernel, chunk),
        grid=(length // tile,),
        in_specs=[rows, rows, whole((d, wide)), whole((1, wide)), whole((wide, d)), whole((2, d)), whole((2, d)), rows, rows],
        out_specs=[rows, rows],
        out_shape=[full, full],
        compiler_params=pltpu.CompilerParams(vmem_limit_bytes=VMEM_LIMIT),
        cost_estimate=pl.CostEstimate(flops=8 * length * d * wide, bytes_accessed=4 * length * d * 4, transcendentals=0),
        name="mlp_other",
    )(tok, g, up, upb, down, gains, biases, part, share)


def first_tokens(lens, places):
    first = jnp.zeros_like(places)
    end = lens[0, 0]
    for j in range(1, lens.shape[1]):
        first = jnp.where(places >= end, end, first)
        end = end + lens[0, j]
    return jnp.where(places >= end, places, first)


def turn(block, cosine, sine, sign):
    parts = []
    for h in range(block.shape[0] // HEAD):
        r = h * HEAD
        a = block[r : r + HALF, :]
        b = block[r + HALF : r + ROT, :]
        if sign > 0:
            parts += [a * cosine - b * sine, b * cosine + a * sine]
        else:
            parts += [a * cosine + b * sine, b * cosine - a * sine]
        parts.append(block[r + ROT : r + HEAD, :])
    return jnp.concatenate(parts, axis=0)


def proj_kernel(lens, tok, g, w, bias, ow, gains, biases, freq, qt, q, kt, k, vt, dot_t, do, cosine, sine):
    tile = tok.shape[0]
    i = pl.program_id(0)
    hat, _ = hat_of(tok[...].astype(f32))
    normed = (hat * gains[0:1, :] + biases[0:1, :]).astype(bf16)
    places = i * tile + lax.broadcasted_iota(jnp.int32, (1, tile), 1)
    position = (places - first_tokens(lens, places)).astype(f32)
    theta = freq[:, 0:1] * position
    c = jnp.cos(theta)
    s = jnp.sin(theta)
    cosine[...] = c
    sine[...] = s
    scale = HEAD ** (-0.5)
    query = turn(dot(w[0], normed, TT) + bias[:, 0:1], c, s, 1).astype(bf16) * scale
    qt[...] = query
    q[...] = query.T
    key = turn(dot(w[1], normed, TT), c, s, 1).astype(bf16)
    kt[...] = key
    k[...] = key.T
    vt[...] = (dot(w[2], normed, TT) + bias[:, 1:2]).astype(bf16)
    grad = dot(ow[...], g[...], NT).astype(bf16)
    dot_t[...] = grad
    do[...] = grad.T


def project(lens, tok, g, w, bias, ow, gains, biases, freq, tile=512):
    length, d = tok.shape
    e = w.shape[2]
    rows = pl.BlockSpec((tile, d), lambda i, *_: (i, 0))
    tr = pl.BlockSpec((e, tile), lambda i, *_: (0, i))
    nat = pl.BlockSpec((tile, e), lambda i, *_: (i, 0))
    ang = pl.BlockSpec((HALF, tile), lambda i, *_: (0, i))
    t_shape = jax.ShapeDtypeStruct((e, length), bf16)
    n_shape = jax.ShapeDtypeStruct((length, e), bf16)
    a_shape = jax.ShapeDtypeStruct((HALF, length), f32)
    return pl.pallas_call(
        proj_kernel,
        grid_spec=pltpu.PrefetchScalarGridSpec(
            num_scalar_prefetch=1,
            grid=(length // tile,),
            in_specs=[rows, rows, whole((3, d, e)), whole((e, 2)), whole((e, d)), whole((2, d)), whole((2, d)), whole((HALF, 128))],
            out_specs=[tr, nat, tr, nat, tr, tr, nat, ang, ang],
        ),
        out_shape=[t_shape, n_shape, t_shape, n_shape, t_shape, t_shape, n_shape, a_shape, a_shape],
        compiler_params=pltpu.CompilerParams(vmem_limit_bytes=VMEM_LIMIT),
        cost_estimate=pl.CostEstimate(flops=8 * length * d * e, bytes_accessed=20 * length * e, transcendentals=0),
        name="project",
    )(lens, tok, g, w, bias, ow, gains, biases, freq)


def tile_range(lens, start):
    first = jnp.int32(0)
    end = lens[0, 0]
    for j in range(1, lens.shape[1]):
        first = jnp.where(start >= end, end, first)
        end = end + lens[0, j]
    return jnp.where(start >= end, start, first)


def low_parts(x):
    high = x.astype(bf16)
    rest = x - high.astype(f32)
    mid = rest.astype(bf16)
    return [high, mid, (rest - mid.astype(f32)).astype(bf16)]


def tile_plan(lens, q0, tq, tk):
    low = lax.div(tile_range(lens, q0), tk)
    diagonal = lax.div(q0, tk)
    high = lax.div(q0 + tq + tk - 1, tk)
    inner = jnp.minimum(lax.div(tile_range(lens, q0 + tq - 1) + tk - 1, tk), diagonal)
    return low, jnp.maximum(inner, low), diagonal, high


def over_tiles(lens, q0, tq, tk, step, carry):
    low, inner, diagonal, high = tile_plan(lens, q0, tq, tk)
    edges = inner - low
    masked = lambda t, c: step(jnp.where(t < edges, low + t, diagonal + t - edges), c, True)
    carry = lax.fori_loop(0, edges + high - diagonal, masked, carry)
    return lax.fori_loop(inner, diagonal, lambda j, c: step(j, c, False), carry)


VROWS = 80


def attend_kernel(tk, lens, qt, k, vt, ot, qpad, vpad, acc):
    i = pl.program_id(0)
    tq = qt.shape[1]
    heads = qt.shape[0] // HEAD
    q0 = i * tq

    @pl.when(i == 0)
    def _():
        row = lax.broadcasted_iota(jnp.int32, (VROWS - HEAD, vt.shape[1]), 0)
        ones = jnp.where(row == 0, 1.0, 0.0).astype(bf16)
        for h in range(heads):
            vpad[h, :HEAD, :] = vt[h * HEAD : (h + 1) * HEAD, :]
            vpad[h, HEAD:, :] = ones

    places = q0 + lax.broadcasted_iota(jnp.int32, (1, tq), 1)
    first = first_tokens(lens, places)
    zero = jnp.zeros((HEAD, tq), bf16)
    for h in range(heads):
        qh = qt[h * HEAD : (h + 1) * HEAD, :]
        qpad[h] = jnp.concatenate([qh, zero] if h % 2 == 0 else [zero, qh], axis=0)
    acc[...] = jnp.zeros_like(acc)

    def step(j, peaks, masked):
        k0 = pl.multiple_of(j * tk, tk)
        if masked:
            rows = k0 + lax.broadcasted_iota(jnp.int32, (tk, tq), 0)
            allowed = (rows >= first) & (rows <= places)
        scores, new, raised = [], [], []
        for h in range(heads):
            pair = (h // 2) * 128
            s = dot(k[pl.ds(k0, tk), pair : pair + 128], qpad[h])
            scores.append(jnp.where(allowed, s, -1e30) if masked else s)
        for h in range(heads):
            new.append(jnp.maximum(peaks[h], jnp.max(scores[h], axis=0, keepdims=True)))
            raised.append(jnp.exp(scores[h] - new[h]).astype(bf16))
        for h in range(heads):
            o = dot(vpad[h, :, pl.ds(k0, tk)], raised[h])
            acc[h] = acc[h] * jnp.exp(peaks[h] - new[h]) + o
        return tuple(new)

    start = tuple(jnp.full((1, tq), -1e30, f32) for _ in range(heads))
    peaks = over_tiles(lens, q0, tq, tk, step, start)
    logs = []
    for h in range(heads):
        total = acc[h, HEAD : HEAD + 1, :]
        ot[h * HEAD : (h + 1) * HEAD, :] = acc[h, :HEAD, :] / total
        logs.append(peaks[h] + jnp.log(total))
    logs.append(jnp.zeros((8 - heads, tq), f32))
    ot[heads * HEAD :, :] = jnp.concatenate(logs, axis=0)


def attend(lens, qt, k, vt, tq=256, tk=256):
    e, length = qt.shape
    heads = e // HEAD
    cols = pl.BlockSpec((e, tq), lambda i, *_: (0, i))
    return pl.pallas_call(
        functools.partial(attend_kernel, tk),
        grid_spec=pltpu.PrefetchScalarGridSpec(
            num_scalar_prefetch=1,
            grid=(length // tq,),
            in_specs=[cols, whole((length, e)), whole((e, length))],
            out_specs=pl.BlockSpec((e + 8, tq), lambda i, *_: (0, i)),
            scratch_shapes=[
                pltpu.VMEM((heads, 128, tq), bf16),
                pltpu.VMEM((heads, VROWS, length), bf16),
                pltpu.VMEM((heads, VROWS, tq), f32),
            ],
        ),
        out_shape=jax.ShapeDtypeStruct((e + 8, length), f32),
        compiler_params=pltpu.CompilerParams(vmem_limit_bytes=VMEM_LIMIT),
        cost_estimate=pl.CostEstimate(flops=2 * length * length * e, bytes_accessed=8 * length * e, transcendentals=0),
        name="attend",
    )(lens, qt, k, vt)


def attend_back_kernel(tk, lens, q, qt, k, kt, vt, do, dot_t, ot, cosine, sine, grads_q, grads_k, grads_v, kpad, vpad, dk, dv, dq, qa, da, cs, cd):
    i = pl.program_id(0)
    tq = q.shape[0]
    length = k.shape[0]
    heads = q.shape[1] // HEAD
    q0 = i * tq

    @pl.when(i == 0)
    def _():
        dk[...] = jnp.zeros_like(dk)
        dv[...] = jnp.zeros_like(dv)
        zero = jnp.zeros((HEAD, length), bf16)
        row = lax.broadcasted_iota(jnp.int32, (128, tk), 0)
        for h in range(heads):
            sl = slice(h * HEAD, (h + 1) * HEAD)
            own, other = (0, HEAD) if h % 2 == 0 else (HEAD, 0)
            kpad[h, own : own + HEAD, :] = kt[sl, :]
            kpad[h, other : other + HEAD, :] = zero
            vpad[h, own : own + HEAD, :] = vt[sl, :]
            vpad[h, other : other + HEAD, :] = zero
            cs[h] = jnp.where((row < 24) & (row % 8 == h), -1.0, 0.0).astype(bf16)
            cd[h] = jnp.where((row >= 24) & (row < 48) & (row % 8 == h), -1.0, 0.0).astype(bf16)

    places = q0 + lax.broadcasted_iota(jnp.int32, (tq, 1), 0)
    first = first_tokens(lens, places)
    deltas = [
        jnp.sum(ot[h * HEAD : (h + 1) * HEAD, :] * dot_t[h * HEAD : (h + 1) * HEAD, :].astype(f32), axis=0, keepdims=True)
        for h in range(heads)
    ]
    deltas.append(jnp.zeros((8 - heads, tq), f32))
    stats = low_parts(ot[heads * HEAD :, :]) + low_parts(jnp.concatenate(deltas, axis=0))
    stats.append(jnp.zeros((128 - 48, tq), bf16))
    stat_cols = jnp.concatenate(stats, axis=0).T
    for r in range(heads // 2):
        pair = slice(r * 128, r * 128 + 128)
        qa[r, :, :128] = q[:, pair]
        qa[r, :, 128:] = stat_cols
        da[r, :, :128] = do[:, pair]
        da[r, :, 128:] = stat_cols
    dq[...] = jnp.zeros_like(dq)

    def step(j, carry, masked):
        k0 = pl.multiple_of(j * tk, tk)
        ks = pl.ds(k0, tk)
        if masked:
            cols = k0 + lax.broadcasted_iota(jnp.int32, (tq, tk), 1)
            allowed = (cols >= first) & (cols <= places)
        probs, grads = [], []
        for h in range(heads):
            s = dot(qa[h // 2], jnp.concatenate([kpad[h, :, ks], cs[h]], axis=0))
            dp = dot(da[h // 2], jnp.concatenate([vpad[h, :, ks], cd[h]], axis=0))
            p = jnp.exp(s)
            if masked:
                p = jnp.where(allowed, p, 0.0)
            probs.append(p.astype(bf16))
            grads.append((p * dp).astype(bf16))
        for h in range(heads):
            sl = slice(h * HEAD, (h + 1) * HEAD)
            pair = slice((h // 2) * 128, (h // 2) * 128 + 128)
            dv[sl, ks] += dot(dot_t[sl, :], probs[h])
            dk[sl, ks] += dot(qt[sl, :], grads[h])
            dq[h] += dot(grads[h], k[ks, pair])
        return carry

    over_tiles(lens, q0, tq, tk, step, 0)
    scale = HEAD ** (-0.5)
    lane = lax.broadcasted_iota(jnp.int32, (tq, 128), 1)
    q_parts = [
        jnp.where(lane < HEAD, dq[2 * h], dq[2 * h + 1]).T * scale for h in range(heads // 2)
    ]
    angle = pl.ds(pl.multiple_of(q0, tq), tq)
    grads_q[...] = turn(jnp.concatenate(q_parts, axis=0), cosine[:, angle], sine[:, angle], -1).astype(bf16)

    @pl.when(i == pl.num_programs(0) - 1)
    def _():
        grads_k[...] = turn(dk[...], cosine[...], sine[...], -1).astype(bf16)
        grads_v[...] = dv[...].astype(bf16)


def attend_back(lens, q, qt, k, kt, vt, do, dot_t, ot, cosine, sine, tq=256, tk=256):
    e, length = qt.shape
    heads = e // HEAD
    cols = pl.BlockSpec((e, tq), lambda i, *_: (0, i))
    rows = pl.BlockSpec((tq, e), lambda i, *_: (i, 0))
    stat = pl.BlockSpec((e + 8, tq), lambda i, *_: (0, i))
    nat, tr, ang = whole((length, e)), whole((e, length)), whole((HALF, length))
    out = jax.ShapeDtypeStruct((e, length), bf16)
    return pl.pallas_call(
        functools.partial(attend_back_kernel, tk),
        grid_spec=pltpu.PrefetchScalarGridSpec(
            num_scalar_prefetch=1,
            grid=(length // tq,),
            in_specs=[rows, cols, nat, tr, tr, rows, cols, stat, ang, ang],
            out_specs=[cols, once((e, length)), once((e, length))],
            scratch_shapes=[
                pltpu.VMEM((heads, 128, length), bf16),
                pltpu.VMEM((heads, 128, length), bf16),
                pltpu.VMEM((e, length), f32),
                pltpu.VMEM((e, length), f32),
                pltpu.VMEM((heads, tq, 128), f32),
                pltpu.VMEM((heads // 2, tq, 256), bf16),
                pltpu.VMEM((heads // 2, tq, 256), bf16),
                pltpu.VMEM((heads, 128, tk), bf16),
                pltpu.VMEM((heads, 128, tk), bf16),
            ],
        ),
        out_shape=[out, out, out],
        compiler_params=pltpu.CompilerParams(vmem_limit_bytes=VMEM_LIMIT),
        cost_estimate=pl.CostEstimate(flops=5 * length * length * e, bytes_accessed=20 * length * e, transcendentals=0),
        name="attend_back",
    )(lens, q, qt, k, kt, vt, do, dot_t, ot, cosine, sine)


def merge_tile(tok, gq, gk, gv, ot, w, ow, gains, biases):
    hat, inverse = hat_of(tok[...].astype(f32))
    gain = gains[0:1, :]
    back = dot(gq[...], w[0], TT) + dot(gk[...], w[1], TT) + dot(gv[...], w[2], TT)
    low = ot[...].astype(bf16)
    return hat, inverse, gain, back, low, dot(low, ow[...], TN)


def merge_own_kernel(meta, tok, g, gq, gk, gv, ot, w, ow, gains, biases, part_in, share_in, part, share, keep, send, small, bias_sum, dw, dow):
    i = pl.program_id(0)
    tile = tok.shape[0]

    @pl.when(i == 0)
    def _():
        dw[...] = jnp.zeros_like(dw)
        dow[...] = jnp.zeros_like(dow)
        small[...] = jnp.zeros_like(small)
        bias_sum[...] = jnp.zeros_like(bias_sum)

    hat, _, gain, back, low, out = merge_tile(tok, gq, gk, gv, ot, w, ow, gains, biases)
    normed = (hat * gain + biases[0:1, :]).astype(bf16)
    share[...] = share_in[...] + back * gain
    part[...] = part_in[...] + out
    dw[0] += dot(normed, gq[...], TT)
    dw[1] += dot(normed, gk[...], TT)
    dw[2] += dot(normed, gv[...], TT)
    dow[...] += dot(low, g[...])
    small[0:1, :] += jnp.sum(back * hat, axis=0, keepdims=True)
    small[1:2, :] += jnp.sum(back, axis=0, keepdims=True)
    ones = jnp.ones((8, tile), bf16)
    bias_sum[0] += dot(ones, gq[...], NT)
    bias_sum[1] += dot(ones, gv[...], NT)

    @pl.when(i == pl.num_programs(0) - 1)
    def _():
        _, d, e = dw.shape
        core = meta[0]
        quarter = d // 4
        for ref, half in ((keep, core), (send, 1 - core)):
            for c in range(3):
                for s in range(2):
                    rows = pl.multiple_of(half * (2 * quarter) + s * quarter, quarter)
                    ref[c * quarter : (c + 1) * quarter, s * e : (s + 1) * e] = dw[c, pl.ds(rows, quarter), :]
            rows = pl.multiple_of(half * (e // 2), e // 2)
            ref[3 * quarter :, :] = dow[pl.ds(rows, e // 2), :]


def merge_own(meta, tok, g, gq, gk, gv, ot, w, ow, gains, biases, part, share, tile=512):
    length, d = tok.shape
    e = w.shape[2]
    rows = pl.BlockSpec((tile, d), lambda i, *_: (i, 0))
    cols = pl.BlockSpec((e, tile), lambda i, *_: (0, i))
    full = jax.ShapeDtypeStruct((length, d), f32)
    half = (3 * d // 4 + e // 2, d)
    return pl.pallas_call(
        merge_own_kernel,
        grid_spec=pltpu.PrefetchScalarGridSpec(
            num_scalar_prefetch=1,
            grid=(length // tile,),
            in_specs=[rows, rows, cols, cols, cols, cols, whole((3, d, e)), whole((e, d)), whole((2, d)), whole((2, d)), rows, rows],
            out_specs=[rows, rows, once(half), once(half), once((8, d)), once((2, 8, e))],
            scratch_shapes=[pltpu.VMEM((3, d, e), f32), pltpu.VMEM((e, d), f32)],
        ),
        out_shape=[
            full,
            full,
            jax.ShapeDtypeStruct(half, f32),
            jax.ShapeDtypeStruct(half, f32),
            jax.ShapeDtypeStruct((8, d), f32),
            jax.ShapeDtypeStruct((2, 8, e), f32),
        ],
        compiler_params=pltpu.CompilerParams(vmem_limit_bytes=VMEM_LIMIT),
        cost_estimate=pl.CostEstimate(flops=16 * length * d * e, bytes_accessed=24 * length * d, transcendentals=0),
        name="merge_own",
    )(meta, tok, g, gq, gk, gv, ot, w, ow, gains, biases, part, share)


def merge_other_kernel(tok, g, gq, gk, gv, ot, w, ow, gains, biases, out_bias, part_in, share_in, output, input_grad):
    hat, inverse, gain, back, _, out = merge_tile(tok, gq, gk, gv, ot, w, ow, gains, biases)
    shares = share_in[...] + back * gain
    inputs = tok[...].astype(f32)
    output[...] = (inputs + (part_in[...] + out) + out_bias[0:1, :] + out_bias[1:2, :]).astype(bf16)
    input_share = inverse * (
        shares
        - jnp.mean(shares, axis=-1, keepdims=True)
        - hat * jnp.mean(shares * hat, axis=-1, keepdims=True)
    )
    input_grad[...] = (g[...].astype(f32) + input_share).astype(bf16)


def merge_other(tok, g, gq, gk, gv, ot, w, ow, gains, biases, out_bias, part, share, tile=512):
    length, d = tok.shape
    e = w.shape[2]
    rows = pl.BlockSpec((tile, d), lambda i: (i, 0))
    cols = pl.BlockSpec((e, tile), lambda i: (0, i))
    full = jax.ShapeDtypeStruct((length, d), bf16)
    return pl.pallas_call(
        merge_other_kernel,
        grid=(length // tile,),
        in_specs=[rows, rows, cols, cols, cols, cols, whole((3, d, e)), whole((e, d)), whole((2, d)), whole((2, d)), whole((2, d)), rows, rows],
        out_specs=[rows, rows],
        out_shape=[full, full],
        compiler_params=pltpu.CompilerParams(vmem_limit_bytes=VMEM_LIMIT),
        cost_estimate=pl.CostEstimate(flops=8 * length * d * e, bytes_accessed=24 * length * d, transcendentals=0),
        name="merge_other",
    )(tok, g, gq, gk, gv, ot, w, ow, gains, biases, out_bias, part, share)


def pack_kernel(meta, w, ow, up, down, first, second):
    d = ow.shape[1]
    e = w.shape[2]
    for n, ref in enumerate((first, second)):
        at = 0
        r = down.shape[0] // 2
        ref[at : at + r, :] = down[n * r : (n + 1) * r, :].astype(f32)
        at += r
        r = up.shape[0] // 2
        for c in range(up.shape[1] // d):
            ref[at : at + r, :] = up[n * r : (n + 1) * r, c * d : (c + 1) * d].astype(f32)
            at += r
        r = w.shape[1] // 4
        for c in range(3):
            for s in range(2):
                ref[at : at + r, s * e : (s + 1) * e] = w[c, (2 * n + s) * r : (2 * n + s + 1) * r, :].astype(f32)
            at += r
        r = ow.shape[0] // 2
        ref[at : at + r, :] = ow[n * r : (n + 1) * r, :].astype(f32)


def pack(meta, w, ow, up, down):
    _, d, e = w.shape
    wide = up.shape[1]
    rows = (wide + (wide // d) * d + 3 * d // 2 + e) // 8
    piece = jax.ShapeDtypeStruct((rows, d), f32)
    return pl.pallas_call(
        pack_kernel,
        grid_spec=pltpu.PrefetchScalarGridSpec(
            num_scalar_prefetch=1,
            grid=(1,),
            in_specs=[
                pl.BlockSpec((3, d // 4, e), lambda i, m: (0, m[1], 0)),
                pl.BlockSpec((e // 4, d), lambda i, m: (m[1], 0)),
                pl.BlockSpec((d // 4, wide), lambda i, m: (m[1], 0)),
                pl.BlockSpec((wide // 4, d), lambda i, m: (m[1], 0)),
            ],
            out_specs=[once((rows, d)), once((rows, d))],
        ),
        out_shape=[piece, piece],
        compiler_params=pltpu.CompilerParams(vmem_limit_bytes=VMEM_LIMIT),
        name="pack",
    )(meta, w, ow, up, down)


def unpack_kernel(meta, *refs):
    pieces, (w, ow, up, down) = refs[:8], refs[8:]
    d = ow.shape[1]
    e = w.shape[2]
    for n, ref in enumerate(pieces):
        core = meta[0] ^ (n // 4)
        parity = meta[2] ^ ((n // 2) % 2)
        at_piece = (parity * 2 + core) * 2 + n % 2
        at = 0
        r = down.shape[0] // 8
        down[pl.ds(pl.multiple_of(at_piece * r, r), r), :] = ref[at : at + r, :].astype(bf16)
        at += r
        r = up.shape[0] // 8
        for c in range(up.shape[1] // d):
            up[pl.ds(pl.multiple_of(at_piece * r, r), r), c * d : (c + 1) * d] = ref[at : at + r, :].astype(bf16)
            at += r
        r = w.shape[1] // 16
        for c in range(3):
            for s in range(2):
                w[c, pl.ds(pl.multiple_of((at_piece * 2 + s) * r, r), r), :] = ref[at : at + r, s * e : (s + 1) * e].astype(bf16)
            at += r
        r = ow.shape[0] // 8
        ow[pl.ds(pl.multiple_of(at_piece * r, r), r), :] = ref[at : at + r, :].astype(bf16)


def unpack(meta, pieces, w, ow, up, down):
    shapes = [jax.ShapeDtypeStruct(x.shape, bf16) for x in (w, ow, up, down)]
    return pl.pallas_call(
        unpack_kernel,
        grid_spec=pltpu.PrefetchScalarGridSpec(
            num_scalar_prefetch=1,
            grid=(1,),
            in_specs=[once(p.shape) for p in pieces],
            out_specs=[once(s.shape) for s in shapes],
        ),
        out_shape=shapes,
        compiler_params=pltpu.CompilerParams(vmem_limit_bytes=VMEM_LIMIT),
        name="unpack",
    )(meta, *pieces)


def swap(x, bit):
    n = lax.axis_size("dp")
    return lax.ppermute(x, "dp", [(i, i ^ (1 << bit)) for i in range(n)])


def across(x):
    return lax.ppermute(x, "tensor", [(0, 1), (1, 0)])


def total_over_dp(keep, send, order, me):
    got = swap(send, 0)
    for b in order:
        v = (me >> b) & 1
        r = keep.shape[0] // 2
        part = lambda x, at: lax.dynamic_slice_in_dim(x, at * r, r, 0)
        send = part(keep, 1 - v) + part(got, 1 - v)
        keep = part(keep, v) + part(got, v)
        got = swap(send, b)
    full = keep + got
    for b in reversed(order):
        got = swap(full, b)
        full = in_order((me >> b) & 1, full, got, 0)
    return full


def in_order(v, mine, got, axis):
    return jnp.concatenate([jnp.where(v == 0, mine, got), jnp.where(v == 0, got, mine)], axis=axis)


def small_total(x, bits):
    for b in range(bits):
        x = x + swap(x, b)
    return x


def per_device(
    tokens, lengths, qkv_weight, qkv_bias, out_weight, out_bias, up_weight, up_bias, down_weight, down_bias, norm_gains, norm_biases, cotangent
):
    length, d = tokens.shape
    e = qkv_weight.shape[2]
    wide = up_weight.shape[1]
    size = lax.axis_size("dp")
    bits = size.bit_length() - 1
    me = lax.axis_index("dp")
    core = me & 1
    parity = ((me >> 1) ^ (me >> 2)) & 1
    meta = jnp.stack([core, parity * 2 + core, parity] + [jnp.int32(0)] * 5)
    freq = jnp.broadcast_to(
        (rot_base ** (-(2.0 * jnp.arange(HALF, dtype=f32)) / ROT))[:, None], (HALF, 128)
    )
    first, second = pack(meta, qkv_weight, out_weight, up_weight, down_weight)
    own_biases = jnp.concatenate([up_bias.astype(f32), qkv_bias.astype(f32).reshape(-1)]).reshape(-1, d)
    other_biases = across(own_biases)
    first, second = across(first), across(second)
    near = [first, second, swap(first, 1), swap(second, 2)]
    pieces = near + [swap(x, 0) for x in near]
    other_w, other_ow, other_up, other_down = unpack(meta, pieces, qkv_weight, out_weight, up_weight, down_weight)

    def half_biases(rows):
        flat = rows.reshape(-1)
        return flat[None, :wide], flat[wide:].reshape(2, e).T

    own_upb, own_qkvb = half_biases(own_biases)
    other_upb, other_qkvb = half_biases(other_biases)
    part, share, keep_d, send_d, keep_u, send_u, small_a, d_upb = mlp_own(
        meta, tokens, cotangent, up_weight, own_upb, down_weight, norm_gains, norm_biases
    )
    order = list(range(1, bits))
    turned = order[1:] + order[:1]
    half_d = total_over_dp(keep_d, send_d, order, me)
    half_u = total_over_dp(keep_u, send_u, turned, me)
    part, share, lengths_b = lax.optimization_barrier((part, share, lengths))
    qt, q, kt, k, vt, dot_t, do, cosine, sine = project(
        lengths_b, tokens, cotangent, qkv_weight, own_qkvb, out_weight, norm_gains, norm_biases, freq
    )
    ot = attend(lengths, qt, k, vt)
    other_ot = across(ot)
    gq, gk, gv = attend_back(lengths, q, qt, k, kt, vt, do, dot_t, ot, cosine, sine)
    part, share, keep_a, send_a, small_b, bias_sum = merge_own(
        meta, tokens, cotangent, gq, gk, gv, ot, qkv_weight, out_weight, norm_gains, norm_biases, part, share
    )
    half_a = total_over_dp(keep_a, send_a, order, me)
    norm_sums = jnp.stack([small_b[0], small_a[1], small_b[1], small_a[2]])
    norm_sums = norm_sums + across(norm_sums)
    smalls = jnp.concatenate([norm_sums, small_a[:1], d_upb.reshape(-1, d), bias_sum[:, 0, :].reshape(-1, d)])
    smalls = small_total(smalls, bits)
    part, share, lengths_c = lax.optimization_barrier((part, share, lengths))
    qt, q, kt, k, vt, dot_t, do, cosine, sine = project(
        lengths_c, tokens, cotangent, other_w, other_qkvb, other_ow, norm_gains, norm_biases, freq
    )
    gq, gk, gv = attend_back(lengths, q, qt, k, kt, vt, do, dot_t, other_ot, cosine, sine)
    part, share = mlp_other(tokens, cotangent, other_up, other_upb, other_down, norm_gains, norm_biases, part, share)
    out_biases = jnp.stack([out_bias, down_bias]).astype(f32)
    output, input_grad = merge_other(
        tokens, cotangent, gq, gk, gv, other_ot, other_w, other_ow, norm_gains, norm_biases, out_biases, part, share
    )
    d_down = in_order(core, half_d, swap(half_d, 0), 0)
    d_up = in_order(core, half_u, swap(half_u, 0), 0)
    d_up = d_up.reshape(2, wide // d, d // 2, d).transpose(0, 2, 1, 3).reshape(d, wide)
    d_a = in_order(core, half_a, swap(half_a, 0), 0).reshape(2, -1, d)
    d_qkv = d_a[:, : 3 * d // 4].reshape(2, 3, d // 4, 2, e).transpose(1, 0, 3, 2, 4).reshape(3, d, e)
    d_out = d_a[:, 3 * d // 4 :].reshape(e, d)
    rest = smalls[5:].reshape(-1)
    return (
        output, input_grad, d_qkv, rest[wide:].reshape(2, e), d_out, smalls[4], d_up, rest[:wide], d_down, smalls[4], smalls[:2], smalls[2:4],
    )


def solution(mesh):
    in_specs = (
        P("dp", None), P("dp", None), P(None, None, "tensor"), P(None, "tensor"), P("tensor", None), P(), P(None, "tensor"),
        P("tensor"), P("tensor", None), P(), P(), P(), P("dp", None),
    )
    out_specs = (
        P("dp", None), P("dp", None), P(None, None, "tensor"), P(None, "tensor"), P("tensor", None), P(), P(None, "tensor"),
        P("tensor"), P("tensor", None), P(), P(), P(),
    )
    return jax.shard_map(per_device, mesh=mesh, in_specs=in_specs, out_specs=out_specs, check_vma=False)
```

time: 789 us -> 557 us (0.71); the launches traced: 789 us -> 549 us
  waiting for transfers between devices: 442 us -> 147 us
  blocking collectives: 115 us -> 0 us
  starting transfers between devices: 0.08 us -> 68.5 us
  Pallas kernels: 185 us -> 252 us
  other arithmetic: 13.9 us -> 47.4 us
  local copies, waits for them, and re-layouts: 19.7 us -> 32.4 us
  between operations: 14.2 us -> 1.57 us
    psum x2 -> x0, waiting for transfers between devices: 441 us -> none  [the longest x1 251 us: per_device(): lax.psum((d_qkv, d_qkvb, d_out, d_up, d_upb, d_down, bias_grad), 'dp')]
    ppermute x0 -> x39, waiting for transfers between devices: none -> 147 us  [the longest x34 130 us: swap(): return lax.ppermute(x, 'dp', [(i, i ^ 1 << bit) for i in range(n)])]
    psum x2 -> x0, blocking collectives: 115 us -> none  [the longest x1 77 us: per_device(): lax.psum((d_qkv, d_qkvb, d_out, d_up, d_upb, d_down, bias_grad), 'dp')]
    ppermute x0 -> x39, starting transfers between devices: none -> 68.5 us  [the longest x34 60.5 us: swap(): return lax.ppermute(x, 'dp', [(i, i ^ 1 << bit) for i in range(n)])]
    pallas_call x2 -> x6, Pallas kernels: 69.1 us -> 132 us  [the longest x1 48 us: mlp_own(): pl.pallas_call(functools.partial(mlp_own_kernel, chunk), grid_spec=pltpu....]
    pallas_call x1, Pallas kernels: 46 us -> 23.1 us  [attend(): pl.pallas_call(functools.partial(attend_kernel, tk), grid_spec=pltpu.Pref...]
    add x0 -> x17, other arithmetic: none -> 22.6 us  [the longest x6 17.4 us: total_over_dp(): keep = part(keep, v) + part(got, v)]
    pallas_call x1 -> x2, Pallas kernels: 58 us -> 72.5 us  [attend_back(): pl.pallas_call(functools.partial(attend_back_kernel, tk), grid_spec=pltpu...]
  transfers between devices with their start and end apart: 2 -> 39, of which waited for: 2 -> 16; matrix products, arithmetic and copies ran while one was open for 2% -> 12% of each run, Pallas kernels for 0% -> 37%
where the time goes in v2:
time: 557 us; the launch traced here: 549 us
  Pallas kernels  252 us (45%)
  waiting for transfers between devices  147 us (26%)
  starting transfers between devices  68.5 us (12%)
  other arithmetic  47.4 us (9%)
  local copies, waits for them, and re-layouts  32.4 us (6%)
    ppermute x34, waiting for transfers between devices, swap(): return lax.ppermute(x, 'dp', [(i, i ^ 1 << bit) for i in range(n)])  130 us
    pallas_call x2, Pallas kernels, attend_back(): pl.pallas_call(functools.partial(attend_back_kernel, tk), grid_spec=pltpu...  72.5 us
    ppermute x34, starting transfers between devices, swap(): return lax.ppermute(x, 'dp', [(i, i ^ 1 << bit) for i in range(n)])  60.5 us
    pallas_call x1, Pallas kernels, mlp_own(): pl.pallas_call(functools.partial(mlp_own_kernel, chunk), grid_spec=pltpu....  48 us
    pallas_call x1, Pallas kernels, mlp_other(): pl.pallas_call(functools.partial(mlp_other_kernel, chunk), grid=(length /...  30 us
    pallas_call x2, Pallas kernels, project(): pl.pallas_call(proj_kernel, grid_spec=pltpu.PrefetchScalarGridSpec(num_sc...  24.4 us
    pallas_call x1, Pallas kernels, merge_own(): pl.pallas_call(merge_own_kernel, grid_spec=pltpu.PrefetchScalarGridSpec(n...  24.1 us
    pallas_call x1, Pallas kernels, attend(): pl.pallas_call(functools.partial(attend_kernel, tk), grid_spec=pltpu.Pref...  23.1 us
  transfers between devices with their start and end apart: 39, of which 16 were waited for; matrix products, arithmetic and copies ran while one was open for 12% of the time, Pallas kernels for 37%

profile of v2, /device:TPU:0, one launch (start us, length us, event | category | flops | bytes accessed | tf_op | source)
XLA Modules:
  0.0 548.8 jit_solution(846525721086353291)
XLA Ops:
  0.7 1.3 broadcast_in_dim.14.upb
  2.6 48.0 %mlp_own.1 = (f32[2048,768]{1,0:T(8,128)}, f32[2048,768]{1,0:T(8,128)}, f32[768,768]{1,0:T(8,128)}, f32[768,768]{1,0:T(8,128)}, f32[768,768]{1,0:T(8,128)}, /*in...) custom-call(s32[8]{0:T(128)} %stack.27.meta, bf16[2048,768]{1,0:T(8,128)(2,1)} %tok.11, bf16[2048,768]{1,0:T(8,128)(2,1)} %g.11, ...), custom_call_target="tpu_custom_call" | custom-call | flops 28991029248 | bytes 25165824 | tf_op jit(solution)/shard_map/mlp_own/pallas_call | solution.py:132
  52.7 12.4 %project.2 = (bf16[384,2048]{1,0:T(8,128)(2,1)}, bf16[2048,384]{1,0:T(8,128)(2,1)}, bf16[384,2048]{1,0:T(8,128)(2,1)}, bf16[2048,384]{1,0:T(8,128)(2,1)}, bf16[3...) custom-call(s32[1,8]{1,0:T(1,128)} %lens.7, ...), custom_call_target="tpu_custom_call" | custom-call | flops 4831838208 | bytes 15728640 | tf_op jit(solution)/shard_map/project/pallas_call | solution.py:239
  65.1 23.1 %attend.1.ot = f32[392,2048]{1,0:T(8,128)} custom-call(s32[1,8]{1,0:T(1,128)} %lens.7, bf16[384,2048]{1,0:T(8,128)(2,1)} %get-tuple-element.70.qt, bf16[2048,384]{1,0:T(8,128)(2,1)} %get-tuple-element.71.k, bf16[384,2048]{1,0:T(8,128)(2,1)} %get-tuple-element.73.vt), custom_call_target="tpu_custom_call" | custom-call | flops 3221225472 | bytes 6291456 | tf_op jit(solution)/shard_map/attend/pallas_call | solution.py:344
  88.2 36.1 %attend_back.2 = (bf16[384,2048]{1,0:T(8,128)(2,1)}, bf16[384,2048]{1,0:T(8,128)(2,1)}, bf16[384,2048]{1,0:T(8,128)(2,1)}) custom-call(s32[1,8]{1,0:T(1,128)} %lens.7, bf16[2048,384]{1,0:T(8,128)(2,1)} %get-tuple-element.69.q, bf16[384,2048]{1,0:T(8,128)(2,1)} %get-tuple-element.70.qt, bf16[2048,384]{1,0:T(8,128)(2,1)} %get-tuple-element.71.k, ...), custom_call_target="tpu_custom_call" | custom-call | flops 8053063680 | bytes 15728640 | tf_op jit(solution)/shard_map/attend_back/pallas_call | solution.py:451
  124.4 24.1 %merge_own.1 = (f32[2048,768]{1,0:T(8,128)}, f32[2048,768]{1,0:T(8,128)}, f32[768,768]{1,0:T(8,128)}, f32[768,768]{1,0:T(8,128)}, f32[8,768]{1,0:T(8,128)}, /*index=5*/f32[2,8,384]{2,1,0:T(8,128)}) custom-call(s32[8]{0:T(128)} %stack.27.meta, bf16[2048,768]{1,0:T(8,128)(2,1)} %tok.11, bf16[2048,768]{1,0:T(8,128)(2,1)} %g.11, ...), custom_call_target="tpu_custom_call" | custom-call | flops 9663676416 | bytes 37748736 | tf_op jit(solution)/shard_map/merge_own/pallas_call | solution.py:531
  150.4 2.9 collective-permute-start.18
  155.6 3.7 dynamic-slice_add_fusion.1
  159.3 2.1 collective-permute-start.32
  161.5 4.0 pack.1
  165.5 1.5 collective-permute-start
  168.4 1.3 copy-done.12
  169.7 3.8 dynamic-slice_add_fusion.3
  173.5 1.6 collective-permute-start.24
  175.1 2.9 dynamic-slice_add_fusion.5
  178.0 10.8 %collective-permute-done.20 = f32[8,768]{1,0:T(8,128)S(1)} collective-permute-done((f32[8,768]{1,0:T(8,128)S(1)}, f32[8,768]{1,0:T(8,128)S(1)}, u32[]{:S(2)}, u32[]{:S(2)}) %collective-permute-start.20) | collective-permute-done | bytes 24608 | tf_op jit(solution)/shard_map/ppermute | solution.py:673
  189.4 1.7 collective-permute-start.11
  192.0 1.6 collective-permute-start.21
  193.6 2.5 dynamic-slice_add_fusion.7
  196.1 5.7 %collective-permute-done.21 = f32[8,768]{1,0:T(8,128)S(1)} collective-permute-done((f32[8,768]{1,0:T(8,128)S(1)}, f32[8,768]{1,0:T(8,128)S(1)}, u32[]{:S(2)}, u32[]{:S(2)}) %collective-permute-start.21) | collective-permute-done | bytes 24608 | tf_op jit(solution)/shard_map/ppermute | solution.py:673
  202.4 1.6 collective-permute-start.33
  206.1 1.6 collective-permute-start.8
  207.6 2.2 dynamic-slice_add_fusion.9
  209.8 7.8 %collective-permute-done.11 = f32[384,768]{1,0:T(8,128)} collective-permute-done((f32[384,768]{1,0:T(8,128)}, f32[384,768]{1,0:T(8,128)}, u32[]{:S(2)}, u32[]{:S(2)}) %collective-permute-start.11) | collective-permute-done | bytes 1179680 | tf_op jit(solution)/shard_map/ppermute | solution.py:673
  217.7 3.6 collective-permute-start.25
  221.3 2.3 dynamic-slice_add_fusion.11
  223.6 4.7 collective-permute-start.22
  228.3 16.3 %collective-permute-done.8 = f32[3,768]{1,0:T(4,128)S(1)} collective-permute-done((f32[3,768]{1,0:T(4,128)S(1)}, f32[3,768]{1,0:T(4,128)S(1)}, u32[]{:S(2)}, u32[]{:S(2)}) %collective-permute-start.8) | collective-permute-done | bytes 9248 | tf_op jit(solution)/shard_map/ppermute | solution.py:677
  244.6 1.6 collective-permute-start.12
  247.1 10.5 %collective-permute-start.34 = (f32[96,768]{1,0:T(8,128)S(1)}, f32[96,768]{1,0:T(8,128)S(1)}, u32[]{:S(2)}, u32[]{:S(2)}) collective-permute-start(f32[96,768]{1,0:T(8,128)S(1)} %dynamic-slice_add_fusion.12), channel_id=1, source_target_pairs={{0,16},{2,18},{4,20},{6,22},{8,24},{10,26},{12,28},{14,30},{16,0},... | collective-permute-start | bytes 884744 | tf_op jit(solution)/shard_map/ppermute | solution.py:673
  261.4 5.1 collective-permute-done.34
  267.4 9.9 %collective-permute-start.35 = (f32[96,768]{1,0:T(8,128)S(1)}, f32[96,768]{1,0:T(8,128)S(1)}, u32[]{:S(2)}, u32[]{:S(2)}) collective-permute-start(f32[96,768]{1,0:T(8,128)S(1)} %add_add_fusion), channel_id=1, source_target_pairs={{0,16},{2,18},{4,20},{6,22},{8,24},{10,26},{12,28},{14,30},{16,0},... | collective-permute-start | bytes 884744 | tf_op jit(solution)/shard_map/ppermute | solution.py:673
  277.4 26.2 %collective-permute-done.26 = f32[96,768]{1,0:T(8,128)S(1)} collective-permute-done((f32[96,768]{1,0:T(8,128)S(1)}, f32[96,768]{1,0:T(8,128)S(1)}, u32[]{:S(2)}, u32[]{:S(2)}) %collective-permute-start.26) | collective-permute-done | bytes 294944 | tf_op jit(solution)/shard_map/ppermute | solution.py:673
  305.0 5.8 %collective-permute-done.35 = f32[96,768]{1,0:T(8,128)S(1)} collective-permute-done((f32[96,768]{1,0:T(8,128)S(1)}, f32[96,768]{1,0:T(8,128)S(1)}, u32[]{:S(2)}, u32[]{:S(2)}) %collective-permute-start.35) | collective-permute-done | bytes 294944 | tf_op jit(solution)/shard_map/ppermute | solution.py:673
  311.4 4.2 collective-permute-done.13
  315.6 12.7 %collective-permute-start.36 = (f32[192,768]{1,0:T(8,128)S(1)}, f32[192,768]{1,0:T(8,128)S(1)}, u32[]{:S(2)}, u32[]{:S(2)}) collective-permute-start(f32[192,768]{1,0:T(8,128)S(1)} %pad_maximum_fusion.11), channel_id=1, source_target_pairs={{0,8},{2,10},{4,12},{6,14},{8,0},{10,2},{12,4},{14,6},{16,24},{18,... | collective-permute-start | bytes 1769480 | tf_op jit(solution)/shard_map/ppermute | solution.py:673
  329.9 15.8 %collective-permute-done.14 = f32[96,768]{1,0:T(8,128)S(1)} collective-permute-done((f32[96,768]{1,0:T(8,128)S(1)}, f32[96,768]{1,0:T(8,128)S(1)}, u32[]{:S(2)}, u32[]{:S(2)}) %collective-permute-start.14) | collective-permute-done | bytes 294944 | tf_op jit(solution)/shard_map/ppermute | solution.py:673
  346.4 2.6 collective-permute-start.28
  350.3 1.4 slice_reduce_fusion
  352.4 23.2 %collective-permute-done.28 = f32[192,768]{1,0:T(8,128)S(1)} collective-permute-done((f32[192,768]{1,0:T(8,128)}, f32[192,768]{1,0:T(8,128)S(1)}, u32[]{:S(2)}, u32[]{:S(2)}) %collective-permute-start.28) | collective-permute-done | bytes 589856 | tf_op jit(solution)/shard_map/ppermute | solution.py:673
  379.0 12.7 %collective-permute-done.15 = f32[192,768]{1,0:T(8,128)S(1)} collective-permute-done((f32[192,768]{1,0:T(8,128)S(1)}, f32[192,768]{1,0:T(8,128)S(1)}, u32[]{:S(2)}, u32[]{:S(2)}) %collective-permute-start.15) | collective-permute-done | bytes 589856 | tf_op jit(solution)/shard_map/ppermute | solution.py:673
  391.7 1.5 collective-permute-start.9
  393.4 1.2 pad_maximum_fusion.6
  395.4 1.5 collective-permute-start.16
  396.9 9.4 %unpack.1 = (bf16[3,768,384]{2,1,0:T(8,128)(2,1)}, bf16[384,768]{1,0:T(8,128)(2,1)}, bf16[768,1536]{1,0:T(8,128)(2,1)}, bf16[1536,768]{1,0:T(8,128)(2,1)}) custom-call(s32[8]{0:T(128)} %stack.27.meta, f32[576,768]{1,0:T(8,128)} %collective-permute-done.refs_0_, f32[576,768]{1,0:T(8,128)} %collective-permute-done.1.refs_1_, ...), custom_call_target="tpu_custom_call" | custom-call | tf_op jit(solution)/shard_map/unpack/pallas_call | solution.py:657
  406.3 30.0 %mlp_other.1 = (f32[2048,768]{1,0:T(8,128)}, f32[2048,768]{1,0:T(8,128)}) custom-call(bf16[2048,768]{1,0:T(8,128)(2,1)} %tok.11, bf16[2048,768]{1,0:T(8,128)(2,1)} %g.11, bf16[768,1536]{1,0:T(8,128)(2,1)} %get-tuple-element.102.up, f32[1,1536]{1,0:T(1,128)} %bitcast.32, bf16[1536,768]{1,0:T(8,128)(2,1)} %get-tuple-element.103.down, f32[2,768]{1,0:T(2,128)} %gains.11, ...), custom_call_target="tpu_custom_call" | custom-call | flops 19327352832 | bytes 25165824 | tf_op jit(solution)/shard_map/mlp_other/pallas_call | solution.py:169
  436.3 10.7 %collective-permute-done.16 = f32[384,768]{1,0:T(8,128)} collective-permute-done((f32[384,768]{1,0:T(8,128)}, f32[384,768]{1,0:T(8,128)}, u32[]{:S(2)}, u32[]{:S(2)}) %collective-permute-start.16) | collective-permute-done | bytes 1179680 | tf_op jit(solution)/shard_map/ppermute | solution.py:673
  447.0 1.8 broadcast_select_fusion.11
  448.7 1.6 pad_maximum_fusion.3
  450.3 11.9 %project.3 = (bf16[384,2048]{1,0:T(8,128)(2,1)}, bf16[2048,384]{1,0:T(8,128)(2,1)}, bf16[384,2048]{1,0:T(8,128)(2,1)}, bf16[2048,384]{1,0:T(8,128)(2,1)}, bf16[3...) custom-call(s32[1,8]{1,0:T(1,128)} %lens.7, ...), custom_call_target="tpu_custom_call" | custom-call | flops 4831838208 | bytes 15728640 | tf_op jit(solution)/shard_map/project/pallas_call | solution.py:239
  462.2 1.6 broadcast_select_fusion.7
  463.8 1.7 pad_maximum_fusion.4
  466.5 1.4 broadcast_select_fusion.9
  467.9 1.8 pad_maximum_fusion.5
  470.2 36.4 %attend_back.3 = (bf16[384,2048]{1,0:T(8,128)(2,1)}, bf16[384,2048]{1,0:T(8,128)(2,1)}, bf16[384,2048]{1,0:T(8,128)(2,1)}) custom-call(s32[1,8]{1,0:T(1,128)} %lens.7, bf16[2048,384]{1,0:T(8,128)(2,1)} %get-tuple-element.90.q, bf16[384,2048]{1,0:T(8,128)(2,1)} %get-tuple-element.91.qt, bf16[2048,384]{1,0:T(8,128)(2,1)} %get-tuple-element.92.k, ...), custom_call_target="tpu_custom_call" | custom-call | flops 8053063680 | bytes 15728640 | tf_op jit(solution)/shard_map/attend_back/pallas_call | solution.py:451
  506.5 16.0 %merge_other.1 = (bf16[2048,768]{1,0:T(8,128)(2,1)}, bf16[2048,768]{1,0:T(8,128)(2,1)}) custom-call(bf16[2048,768]{1,0:T(8,128)(2,1)} %tok.11, bf16[2048,768]{1,0:T(8,128)(2,1)} %g.11, bf16[384,2048]{1,0:T(8,128)(2,1)} %get-tuple-element.99.gq, bf16[384,2048]{1,0:T(8,128)(2,1)} %get-tuple-element.100.gk, bf16[384,2048]{1,0:T(8,128)(2,1)} %get-tuple-element.101.gv, ...), custom_call_target="tpu_custom_call" | custom-call | flops 4831838208 | bytes 37748736 | tf_op jit(solution)/shard_map/merge_other/pallas_call | solution.py:573
  522.6 2.0 broadcast_select_fusion.5
  527.2 2.0 broadcast_select_fusion.3
  529.5 3.6 copy.36
  533.1 2.5 copy.38
  535.6 3.3 reshape.77
  538.9 4.3 copy.35
  543.3 2.0 broadcast_select_fusion.1
  545.3 2.5 pad_maximum_fusion.2
  (162 shorter events, 33.4 us)
Async XLA Ops:
  2.6 48.6 %copy-start.26 = (bf16[2,384]{1,0:T(2,128)(2,1)S(1)}, bf16[2,384]{1,0:T(2,128)(2,1)}, u32[]{:S(2)}) copy-start(bf16[2,384]{1,0:T(2,128)(2,1)} %param.16) | copy-start | bytes 4612
  50.6 105.1 %collective-permute-start.31 = (f32[768,768]{1,0:T(8,128)}, f32[768,768]{1,0:T(8,128)}, u32[]{:S(2)}, u32[]{:S(2)}) collective-permute-start(f32[768,768]{1,0:T(8,128)} %get-tuple-element.119), channel_id=1, source_target_pairs={{0,2},{2,0},{4,6},{6,4},{8,10},{10,8},{12,14},{14,12},{16,18},{18,... | collective-permute-start | bytes 7077896 | tf_op jit(solution)/shard_map/ppermute | solution.py:673
  51.1 117.2 %collective-permute-start.23 = (f32[768,768]{1,0:T(8,128)}, f32[768,768]{1,0:T(8,128)S(1)}, u32[]{:S(2)}, u32[]{:S(2)}) collective-permute-start(f32[768,768]{1,0:T(8,128)} %get-tuple-element.117), channel_id=1, source_target_pairs={{0,2},{2,0},{4,6},{6,4},{8,10},{10,8},{12,14},{14,12},{16,18},{18,... | collective-permute-start | bytes 7077896 | tf_op jit(solution)/shard_map/ppermute | solution.py:673
  124.4 29.7 %copy-start.28 = (f32[1,1536]{1,0:T(1,128)S(1)}, f32[1,1536]{1,0:T(1,128)}, u32[]{:S(2)}) copy-start(f32[1,1536]{1,0:T(1,128)} %get-tuple-element.114) | copy-start | bytes 18436
  148.5 25.0 %collective-permute-start.10 = (f32[768,768]{1,0:T(8,128)}, f32[768,768]{1,0:T(8,128)}, u32[]{:S(2)}, u32[]{:S(2)}) collective-permute-start(f32[768,768]{1,0:T(8,128)} %get-tuple-element.111), channel_id=1, source_target_pairs={{0,2},{2,0},{4,6},{6,4},{8,10},{10,8},{12,14},{14,12},{16,18},{18,... | collective-permute-start | bytes 7077896 | tf_op jit(solution)/shard_map/ppermute | solution.py:673
  150.4 4.6 collective-permute-start.18
  154.0 1.6 copy-start.21
  154.1 1.6 copy-start.20
  155.6 11.4 %collective-permute-start.19 = (f32[8,768]{1,0:T(8,128)}, f32[8,768]{1,0:T(8,128)}, u32[]{:S(2)}, u32[]{:S(2)}) collective-permute-start(f32[8,768]{1,0:T(8,128)} %pad_maximum_fusion.12), channel_id=1, source_target_pairs={{0,2},{2,0},{4,6},{6,4},{8,10},{10,8},{12,14},{14,12},{16,18},{18,... | collective-permute-start | bytes 73736 | tf_op jit(solution)/shard_map/ppermute | solution.py:673
  159.3 32.6 %collective-permute-start.32 = (f32[384,768]{1,0:T(8,128)}, f32[384,768]{1,0:T(8,128)}, u32[]{:S(2)}, u32[]{:S(2)}) collective-permute-start(f32[384,768]{1,0:T(8,128)} %get-tuple-element.125), channel_id=1, source_target_pairs={{0,4},{2,6},{4,0},{6,2},{8,12},{10,14},{12,8},{14,10},{16,20},{18,... | collective-permute-start | bytes 3538952 | tf_op jit(solution)/shard_map/ppermute | solution.py:673
  165.5 92.1 %collective-permute-start = (f32[576,768]{1,0:T(8,128)}, f32[576,768]{1,0:T(8,128)}, u32[]{:S(2)}, u32[]{:S(2)}) collective-permute-start(f32[576,768]{1,0:T(8,128)} %get-tuple-element.86), channel_id=1, source_target_pairs={{0,1},{1,0},{2,3},{3,2},{4,5},{5,4},{6,7},{7,6},{8,9},{9,8},{10,11... | collective-permute-start | bytes 5308424 | tf_op jit(solution)/shard_map/ppermute | solution.py:677
  167.0 91.1 %collective-permute-start.1 = (f32[576,768]{1,0:T(8,128)}, f32[576,768]{1,0:T(8,128)}, u32[]{:S(2)}, u32[]{:S(2)}) collective-permute-start(f32[576,768]{1,0:T(8,128)} %get-tuple-element.87), channel_id=1, source_target_pairs={{0,1},{1,0},{2,3},{3,2},{4,5},{5,4},{6,7},{7,6},{8,9},{9,8},{10,11... | collective-permute-start | bytes 5308424 | tf_op jit(solution)/shard_map/ppermute | solution.py:677
  168.3 9.7 %copy-start.19 = (f32[8,768]{1,0:T(8,128)}, f32[8,768]{1,0:T(8,128)S(1)}, u32[]{:S(2)}) copy-start(f32[8,768]{1,0:T(8,128)S(1)} %fusion.1) | copy-start | bytes 73732
  168.3 20.5 %collective-permute-start.20 = (f32[8,768]{1,0:T(8,128)S(1)}, f32[8,768]{1,0:T(8,128)S(1)}, u32[]{:S(2)}, u32[]{:S(2)}) collective-permute-start(f32[8,768]{1,0:T(8,128)S(1)} %fusion.1), channel_id=1, source_target_pairs={{0,4},{2,6},{4,0},{6,2},{8,12},{10,14},{12,8},{14,10},{16,20},{18,... | collective-permute-start | bytes 73736 | tf_op jit(solution)/shard_map/ppermute | solution.py:673
  169.7 5.4 copy-start.13
  173.5 32.5 %collective-permute-start.24 = (f32[384,768]{1,0:T(8,128)}, f32[384,768]{1,0:T(8,128)}, u32[]{:S(2)}, u32[]{:S(2)}) collective-permute-start(f32[384,768]{1,0:T(8,128)} %get-tuple-element.129), channel_id=1, source_target_pairs={{0,8},{2,10},{4,12},{6,14},{8,0},{10,2},{12,4},{14,6},{16,24},{18,... | collective-permute-start | bytes 3538952 | tf_op jit(solution)/shard_map/ppermute | solution.py:673
  189.4 28.2 %collective-permute-start.11 = (f32[384,768]{1,0:T(8,128)}, f32[384,768]{1,0:T(8,128)}, u32[]{:S(2)}, u32[]{:S(2)}) collective-permute-start(f32[384,768]{1,0:T(8,128)} %get-tuple-element.133), channel_id=1, source_target_pairs={{0,4},{2,6},{4,0},{6,2},{8,12},{10,14},{12,8},{14,10},{16,20},{18,... | collective-permute-start | bytes 3538952 | tf_op jit(solution)/shard_map/ppermute | solution.py:673
  192.0 4.1 copy-start.17
  192.0 9.8 %collective-permute-start.21 = (f32[8,768]{1,0:T(8,128)S(1)}, f32[8,768]{1,0:T(8,128)S(1)}, u32[]{:S(2)}, u32[]{:S(2)}) collective-permute-start(f32[8,768]{1,0:T(8,128)S(1)} %add.157), channel_id=1, source_target_pairs={{0,8},{2,10},{4,12},{6,14},{8,0},{10,2},{12,4},{14,6},{16,24},{18,... | collective-permute-start | bytes 73736 | tf_op jit(solution)/shard_map/ppermute | solution.py:673
  193.6 10.4 %copy-start.24 = (bf16[1536]{0:T(1024)(128)(2,1)S(1)}, bf16[1536]{0:T(1024)(128)(2,1)}, u32[]{:S(2)}) copy-start(bf16[1536]{0:T(1024)(128)(2,1)} %param.20) | copy-start | bytes 9220
  193.6 10.4 %copy-start.27 = (bf16[2,384]{1,0:T(2,128)(2,1)S(1)}, bf16[2,384]{1,0:T(2,128)(2,1)}, u32[]{:S(2)}) copy-start(bf16[2,384]{1,0:T(2,128)(2,1)} %param.16) | copy-start | bytes 4612
  193.6 10.4 %copy-start.29 = (bf16[768]{0:T(1024)(128)(2,1)S(1)}, bf16[768]{0:T(1024)(128)(2,1)}, u32[]{:S(2)}) copy-start(bf16[768]{0:T(1024)(128)(2,1)} %param.18) | copy-start | bytes 4612
  202.4 21.2 %collective-permute-start.33 = (f32[192,768]{1,0:T(8,128)}, f32[192,768]{1,0:T(8,128)S(1)}, u32[]{:S(2)}, u32[]{:S(2)}) collective-permute-start(f32[192,768]{1,0:T(8,128)} %get-tuple-element.137), channel_id=1, source_target_pairs={{0,8},{2,10},{4,12},{6,14},{8,0},{10,2},{12,4},{14,6},{16,24},{18,... | collective-permute-start | bytes 1769480 | tf_op jit(solution)/shard_map/ppermute | solution.py:673
  206.1 17.5 %copy-start.18 = (f32[8,768]{1,0:T(8,128)}, f32[8,768]{1,0:T(8,128)S(1)}, u32[]{:S(2)}) copy-start(f32[8,768]{1,0:T(8,128)S(1)} %add.158) | copy-start | bytes 73732
  206.1 38.5 %collective-permute-start.8 = (f32[3,768]{1,0:T(4,128)S(1)}, f32[3,768]{1,0:T(4,128)S(1)}, u32[]{:S(2)}, u32[]{:S(2)}) collective-permute-start(f32[3,768]{1,0:T(4,128)S(1)} %reshape.74), channel_id=1, source_target_pairs={{0,1},{1,0},{2,3},{3,2},{4,5},{5,4},{6,7},{7,6},{8,9},{9,8},{10,11... | collective-permute-start | bytes 27656 | tf_op jit(solution)/shard_map/ppermute | solution.py:677
  217.7 42.7 %collective-permute-start.25 = (f32[192,768]{1,0:T(8,128)}, f32[192,768]{1,0:T(8,128)}, u32[]{:S(2)}, u32[]{:S(2)}) collective-permute-start(f32[192,768]{1,0:T(8,128)} %get-tuple-element.141), channel_id=1, source_target_pairs={{0,16},{2,18},{4,20},{6,22},{8,24},{10,26},{12,28},{14,30},{16,0},... | collective-permute-start | bytes 1769480 | tf_op jit(solution)/shard_map/ppermute | solution.py:673
  221.3 7.0 %copy-start.11 = (f32[192,768]{1,0:T(8,128)S(1)}, f32[192,768]{1,0:T(8,128)}, u32[]{:S(2)}) copy-start(f32[192,768]{1,0:T(8,128)} %get-tuple-element.136) | copy-start | bytes 1769476
  223.6 23.5 %collective-permute-start.22 = (f32[8,768]{1,0:T(8,128)S(1)}, f32[8,768]{1,0:T(8,128)}, u32[]{:S(2)}, u32[]{:S(2)}) collective-permute-start(f32[8,768]{1,0:T(8,128)S(1)} %add.158), channel_id=1, source_target_pairs={{0,16},{2,18},{4,20},{6,22},{8,24},{10,26},{12,28},{14,30},{16,0},... | collective-permute-start | bytes 73736 | tf_op jit(solution)/shard_map/ppermute | solution.py:673
  244.6 22.8 %collective-permute-start.12 = (f32[192,768]{1,0:T(8,128)}, f32[192,768]{1,0:T(8,128)S(1)}, u32[]{:S(2)}, u32[]{:S(2)}) collective-permute-start(f32[192,768]{1,0:T(8,128)} %get-tuple-element.145), channel_id=1, source_target_pairs={{0,8},{2,10},{4,12},{6,14},{8,0},{10,2},{12,4},{14,6},{16,24},{18,... | collective-permute-start | bytes 1769480 | tf_op jit(solution)/shard_map/ppermute | solution.py:673
  247.1 19.4 %collective-permute-start.34 = (f32[96,768]{1,0:T(8,128)S(1)}, f32[96,768]{1,0:T(8,128)S(1)}, u32[]{:S(2)}, u32[]{:S(2)}) collective-permute-start(f32[96,768]{1,0:T(8,128)S(1)} %dynamic-slice_add_fusion.12), channel_id=1, source_target_pairs={{0,16},{2,18},{4,20},{6,22},{8,24},{10,26},{12,28},{14,30},{16,0},... | collective-permute-start | bytes 884744 | tf_op jit(solution)/shard_map/ppermute | solution.py:673
  257.6 71.8 %collective-permute-start.2 = (f32[576,768]{1,0:T(8,128)}, f32[576,768]{1,0:T(8,128)}, u32[]{:S(2)}, u32[]{:S(2)}) collective-permute-start(f32[576,768]{1,0:T(8,128)} %collective-permute-done.refs_0_), channel_id=1, source_target_pairs={{0,4},{2,6},{4,0},{6,2},{8,12},{10,14},{12,8},{14,10},{16,20},{18,... | collective-permute-start | bytes 5308424 | tf_op jit(solution)/shard_map/ppermute | solution.py:673
  258.1 71.3 %collective-permute-start.3 = (f32[576,768]{1,0:T(8,128)}, f32[576,768]{1,0:T(8,128)}, u32[]{:S(2)}, u32[]{:S(2)}) collective-permute-start(f32[576,768]{1,0:T(8,128)} %collective-permute-done.1.refs_1_), channel_id=1, source_target_pairs={{0,8},{2,10},{4,12},{6,14},{8,0},{10,2},{12,4},{14,6},{16,24},{18,... | collective-permute-start | bytes 5308424 | tf_op jit(solution)/shard_map/ppermute | solution.py:673
  260.4 88.7 %copy-start.16 = (f32[8,768]{1,0:T(8,128)}, f32[8,768]{1,0:T(8,128)S(1)}, u32[]{:S(2)}) copy-start(f32[8,768]{1,0:T(8,128)S(1)} %add.159) | copy-start | bytes 73732
  260.4 134.2 %collective-permute-start.4 = (f32[576,768]{1,0:T(8,128)}, f32[576,768]{1,0:T(8,128)}, u32[]{:S(2)}, u32[]{:S(2)}) collective-permute-start(f32[576,768]{1,0:T(8,128)} %collective-permute-done.refs_0_), channel_id=1, source_target_pairs={{0,2},{2,0},{4,6},{6,4},{8,10},{10,8},{12,14},{14,12},{16,18},{18,... | collective-permute-start | bytes 5308424 | tf_op jit(solution)/shard_map/ppermute | solution.py:673
  266.5 37.1 %collective-permute-start.26 = (f32[96,768]{1,0:T(8,128)S(1)}, f32[96,768]{1,0:T(8,128)S(1)}, u32[]{:S(2)}, u32[]{:S(2)}) collective-permute-start(f32[96,768]{1,0:T(8,128)S(1)} %dynamic-slice_add_fusion.13), channel_id=1, source_target_pairs={{0,4},{2,6},{4,0},{6,2},{8,12},{10,14},{12,8},{14,10},{16,20},{18,... | collective-permute-start | bytes 884744 | tf_op jit(solution)/shard_map/ppermute | solution.py:673
  267.4 43.4 %collective-permute-start.35 = (f32[96,768]{1,0:T(8,128)S(1)}, f32[96,768]{1,0:T(8,128)S(1)}, u32[]{:S(2)}, u32[]{:S(2)}) collective-permute-start(f32[96,768]{1,0:T(8,128)S(1)} %add_add_fusion), channel_id=1, source_target_pairs={{0,16},{2,18},{4,20},{6,22},{8,24},{10,26},{12,28},{14,30},{16,0},... | collective-permute-start | bytes 884744 | tf_op jit(solution)/shard_map/ppermute | solution.py:673
  303.6 12.0 %collective-permute-start.13 = (f32[96,768]{1,0:T(8,128)S(1)}, f32[96,768]{1,0:T(8,128)S(1)}, u32[]{:S(2)}, u32[]{:S(2)}) collective-permute-start(f32[96,768]{1,0:T(8,128)S(1)} %dynamic-slice_add_fusion.14), channel_id=1, source_target_pairs={{0,16},{2,18},{4,20},{6,22},{8,24},{10,26},{12,28},{14,30},{16,0},... | collective-permute-start | bytes 884744 | tf_op jit(solution)/shard_map/ppermute | solution.py:673
  310.8 17.6 %collective-permute-start.27 = (f32[96,768]{1,0:T(8,128)S(1)}, f32[96,768]{1,0:T(8,128)S(1)}, u32[]{:S(2)}, u32[]{:S(2)}) collective-permute-start(f32[96,768]{1,0:T(8,128)S(1)} %add_add_fusion.1), channel_id=1, source_target_pairs={{0,4},{2,6},{4,0},{6,2},{8,12},{10,14},{12,8},{14,10},{16,20},{18,... | collective-permute-start | bytes 884744 | tf_op jit(solution)/shard_map/ppermute | solution.py:673
  315.6 30.8 %collective-permute-start.36 = (f32[192,768]{1,0:T(8,128)S(1)}, f32[192,768]{1,0:T(8,128)S(1)}, u32[]{:S(2)}, u32[]{:S(2)}) collective-permute-start(f32[192,768]{1,0:T(8,128)S(1)} %pad_maximum_fusion.11), channel_id=1, source_target_pairs={{0,8},{2,10},{4,12},{6,14},{8,0},{10,2},{12,4},{14,6},{16,24},{18,... | collective-permute-start | bytes 1769480 | tf_op jit(solution)/shard_map/ppermute | solution.py:673
  328.4 17.3 %collective-permute-start.14 = (f32[96,768]{1,0:T(8,128)S(1)}, f32[96,768]{1,0:T(8,128)S(1)}, u32[]{:S(2)}, u32[]{:S(2)}) collective-permute-start(f32[96,768]{1,0:T(8,128)S(1)} %add_add_fusion.2), channel_id=1, source_target_pairs={{0,16},{2,18},{4,20},{6,22},{8,24},{10,26},{12,28},{14,30},{16,0},... | collective-permute-start | bytes 884744 | tf_op jit(solution)/shard_map/ppermute | solution.py:673
  329.4 65.7 %collective-permute-start.5 = (f32[576,768]{1,0:T(8,128)}, f32[576,768]{1,0:T(8,128)}, u32[]{:S(2)}, u32[]{:S(2)}) collective-permute-start(f32[576,768]{1,0:T(8,128)} %collective-permute-done.1.refs_1_), channel_id=1, source_target_pairs={{0,2},{2,0},{4,6},{6,4},{8,10},{10,8},{12,14},{14,12},{16,18},{18,... | collective-permute-start | bytes 5308424 | tf_op jit(solution)/shard_map/ppermute | solution.py:673
  329.4 66.0 %collective-permute-start.6 = (f32[576,768]{1,0:T(8,128)}, f32[576,768]{1,0:T(8,128)}, u32[]{:S(2)}, u32[]{:S(2)}) collective-permute-start(f32[576,768]{1,0:T(8,128)} %collective-permute-done.2.refs_2_), channel_id=1, source_target_pairs={{0,2},{2,0},{4,6},{6,4},{8,10},{10,8},{12,14},{14,12},{16,18},{18,... | collective-permute-start | bytes 5308424 | tf_op jit(solution)/shard_map/ppermute | solution.py:673
  345.7 51.2 %collective-permute-start.7 = (f32[576,768]{1,0:T(8,128)}, f32[576,768]{1,0:T(8,128)}, u32[]{:S(2)}, u32[]{:S(2)}) collective-permute-start(f32[576,768]{1,0:T(8,128)} %collective-permute-done.3.refs_3_), channel_id=1, source_target_pairs={{0,2},{2,0},{4,6},{6,4},{8,10},{10,8},{12,14},{14,12},{16,18},{18,... | collective-permute-start | bytes 5308424 | tf_op jit(solution)/shard_map/ppermute | solution.py:673
  346.4 29.2 %collective-permute-start.28 = (f32[192,768]{1,0:T(8,128)}, f32[192,768]{1,0:T(8,128)S(1)}, u32[]{:S(2)}, u32[]{:S(2)}) collective-permute-start(f32[192,768]{1,0:T(8,128)} %pad_maximum_fusion.10), channel_id=1, source_target_pairs={{0,16},{2,18},{4,20},{6,22},{8,24},{10,26},{12,28},{14,30},{16,0},... | collective-permute-start | bytes 1769480 | tf_op jit(solution)/shard_map/ppermute | solution.py:673
  376.4 15.3 %collective-permute-start.15 = (f32[192,768]{1,0:T(8,128)S(1)}, f32[192,768]{1,0:T(8,128)S(1)}, u32[]{:S(2)}, u32[]{:S(2)}) collective-permute-start(f32[192,768]{1,0:T(8,128)S(1)} %pad_maximum_fusion.9), channel_id=1, source_target_pairs={{0,8},{2,10},{4,12},{6,14},{8,0},{10,2},{12,4},{14,6},{16,24},{18,... | collective-permute-start | bytes 1769480 | tf_op jit(solution)/shard_map/ppermute | solution.py:673
  377.8 15.5 %copy-start.8 = (f32[192,768]{1,0:T(8,128)}, f32[192,768]{1,0:T(8,128)S(1)}, u32[]{:S(2)}) copy-start(f32[192,768]{1,0:T(8,128)S(1)} %get-tuple-element.149) | copy-start | bytes 1769476
  391.7 78.4 %collective-permute-start.9 = (f32[392,2048]{1,0:T(8,128)}, f32[392,2048]{1,0:T(8,128)}, u32[]{:S(2)}, u32[]{:S(2)}) collective-permute-start(f32[392,2048]{1,0:T(8,128)} %attend.1.ot), channel_id=1, source_target_pairs={{0,1},{1,0},{2,3},{3,2},{4,5},{5,4},{6,7},{7,6},{8,9},{9,8},{10,11... | collective-permute-start | bytes 9633800 | tf_op jit(solution)/shard_map/ppermute | solution.py:677
  393.3 12.9 %copy-start.9 = (f32[192,768]{1,0:T(8,128)}, f32[192,768]{1,0:T(8,128)S(1)}, u32[]{:S(2)}) copy-start(f32[192,768]{1,0:T(8,128)S(1)} %get-tuple-element.150) | copy-start | bytes 1769476
  393.3 12.9 %copy-start.10 = (f32[192,768]{1,0:T(8,128)}, f32[192,768]{1,0:T(8,128)S(1)}, u32[]{:S(2)}) copy-start(f32[192,768]{1,0:T(8,128)S(1)} %get-tuple-element.151) | copy-start | bytes 1769476
  394.6 71.9 %collective-permute-start.37 = (f32[384,768]{1,0:T(8,128)}, f32[384,768]{1,0:T(8,128)}, u32[]{:S(2)}, u32[]{:S(2)}) collective-permute-start(f32[384,768]{1,0:T(8,128)} %pad_maximum_fusion.8), channel_id=1, source_target_pairs={{0,4},{2,6},{4,0},{6,2},{8,12},{10,14},{12,8},{14,10},{16,20},{18,... | collective-permute-start | bytes 3538952 | tf_op jit(solution)/shard_map/ppermute | solution.py:673
  395.1 67.2 %collective-permute-start.29 = (f32[384,768]{1,0:T(8,128)}, f32[384,768]{1,0:T(8,128)}, u32[]{:S(2)}, u32[]{:S(2)}) collective-permute-start(f32[384,768]{1,0:T(8,128)} %pad_maximum_fusion.7), channel_id=1, source_target_pairs={{0,8},{2,10},{4,12},{6,14},{8,0},{10,2},{12,4},{14,6},{16,24},{18,... | collective-permute-start | bytes 3538952 | tf_op jit(solution)/shard_map/ppermute | solution.py:673
  395.4 51.6 %collective-permute-start.16 = (f32[384,768]{1,0:T(8,128)}, f32[384,768]{1,0:T(8,128)}, u32[]{:S(2)}, u32[]{:S(2)}) collective-permute-start(f32[384,768]{1,0:T(8,128)} %pad_maximum_fusion.6), channel_id=1, source_target_pairs={{0,4},{2,6},{4,0},{6,2},{8,12},{10,14},{12,8},{14,10},{16,20},{18,... | collective-permute-start | bytes 3538952 | tf_op jit(solution)/shard_map/ppermute | solution.py:673
  450.3 72.3 %collective-permute-start.17 = (f32[768,768]{1,0:T(8,128)}, f32[768,768]{1,0:T(8,128)}, u32[]{:S(2)}, u32[]{:S(2)}) collective-permute-start(f32[768,768]{1,0:T(8,128)} %pad_maximum_fusion.3), channel_id=1, source_target_pairs={{0,2},{2,0},{4,6},{6,4},{8,10},{10,8},{12,14},{14,12},{16,18},{18,... | collective-permute-start | bytes 7077896 | tf_op jit(solution)/shard_map/ppermute | solution.py:673
  463.8 1.8 copy-start.4
  463.8 2.1 copy-start.6
  466.0 60.2 %collective-permute-start.30 = (f32[768,768]{1,0:T(8,128)}, f32[768,768]{1,0:T(8,128)}, u32[]{:S(2)}, u32[]{:S(2)}) collective-permute-start(f32[768,768]{1,0:T(8,128)} %pad_maximum_fusion.4), channel_id=1, source_target_pairs={{0,2},{2,0},{4,6},{6,4},{8,10},{10,8},{12,14},{14,12},{16,18},{18,... | collective-permute-start | bytes 7077896 | tf_op jit(solution)/shard_map/ppermute | solution.py:673
  467.9 1.8 copy-start
  467.9 2.2 copy-start.2
  470.1 73.1 %collective-permute-start.38 = (f32[768,768]{1,0:T(8,128)}, f32[768,768]{1,0:T(8,128)}, u32[]{:S(2)}, u32[]{:S(2)}) collective-permute-start(f32[768,768]{1,0:T(8,128)} %pad_maximum_fusion.5), channel_id=1, source_target_pairs={{0,2},{2,0},{4,6},{6,4},{8,10},{10,8},{12,14},{14,12},{16,18},{18,... | collective-permute-start | bytes 7077896 | tf_op jit(solution)/shard_map/ppermute | solution.py:673
  525.1 1.7 copy-start.5
  525.1 2.0 copy-start.7
  538.9 4.3 copy-start.1
  538.9 4.3 copy-start.3
  545.2 2.5 copy-start.25
  (5 other events, 4.7 us)
